TPU v7x, 256 devices: a whole 4x4x8 slice. The times are simulated.
256 devices in a mesh: dom: 32 (over x, z), tp: 8 (over y, core).
Axes of the slice: x: 4, y: 4, z: 8, core: 2. Of those that a mesh axis runs over, the one named last changes fastest.
Arguments:
- queries: bfloat16 [512, 4, 8192], P('dom', None, 'tp'), may hold values from -100 to 100
- new_keys: bfloat16 [512, 4, 1024], P('dom', None, 'tp'), may hold values from -4 to 4
- new_values: bfloat16 [512, 4, 1024], P('dom', None, 'tp'), may hold values from -4 to 4
- prompt_keys: bfloat16 [2048, 1024], P(None, 'tp'), may hold values from -4 to 4
- prompt_values: bfloat16 [2048, 1024], P(None, 'tp'), may hold values from -4 to 4
- suffix_cache: bfloat16 [512, 2, 256, 1024], P('dom', None, None, 'tp'), may hold values from -4 to 4
- lengths: int32 [512], P('dom'), may hold values from 1 to 252
- ancestors: int32 [512], P('dom'), may hold values from 0 to 511, as said below
- out_weight: bfloat16 [8192, 4096], P('tp'), may hold values from -0.0625 to 0.0625
Outputs:
- mixed: bfloat16 [512, 4, 4096], P('dom', None, 'tp')
- new_cache: bfloat16 [512, 2, 256, 1024], P('dom', None, None, 'tp')
Inputs may be any that keep to these rules, and one draw needn't show every extreme that they name: |ancestors[c] - c| <= 8 for every particle c.
All inputs are finite; a program needn't handle non-finite values.
Results may differ from a plain program's by a relative error of at most 0.019.
Values may be sent and summed in bfloat16 or wider, within the bound.
No kernel may reach another device: no remote copies, remote signals or barrier semaphores. Data moves between devices by JAX's collectives and lax.ppermute only.
A program may use at most 64 MiB of HBM per device.

v0:
```python
import math

import jax
import jax.numpy as jnp
from jax import lax
from jax.sharding import PartitionSpec as P

HD = 128


def padded(value, sides, width):
    for axis, dim in sides:
        count, length = (lax.axis_size(axis), value.shape[dim])
        up = [(i, (i + 1) % count) for i in range(count - 1)]
        down = [(j, i) for i, j in up]
        last = lax.slice_in_dim(value, length - width, length, axis=dim)
        leading = lax.slice_in_dim(value, 0, width, axis=dim)
        before = lax.ppermute(last, axis, up)
        after = lax.ppermute(leading, axis, down)
        value = jnp.concatenate([before, value, after], axis=dim)
    return value


def body(
    queries,
    new_keys,
    new_values,
    prompt_keys,
    prompt_values,
    suffix_cache,
    lengths,
    ancestors,
    out_weight,
):
    part_rows, steps, q_cols = queries.shape
    kv_cols = new_keys.shape[2]
    kv_heads = kv_cols // HD
    group = q_cols // kv_cols
    suffix_len = suffix_cache.shape[2]
    prompt_len = prompt_keys.shape[0]
    scale = 1.0 / math.sqrt(HD)
    query_heads = queries.reshape(part_rows, steps, kv_heads, group, HD)
    prompt_k = prompt_keys.reshape(prompt_len, kv_heads, HD)
    prompt_v = prompt_values.reshape(prompt_len, kv_heads, HD)
    cache_k = suffix_cache[:, 0].reshape(part_rows, suffix_len, kv_heads, HD)
    cache_v = suffix_cache[:, 1].reshape(part_rows, suffix_len, kv_heads, HD)
    fresh_k = new_keys.reshape(part_rows, steps, kv_heads, HD)
    fresh_v = new_values.reshape(part_rows, steps, kv_heads, HD)

    def score_one(query_block):
        return jnp.einsum(
            "sgqd,tgd->gqst", query_block, prompt_k, preferred_element_type=jnp.float32
        )

    prompt_scores = lax.map(score_one, query_heads)
    prompt_scores = prompt_scores * scale
    suffix_scores = (
        jnp.einsum("psgqd,pjgd->pgqsj", query_heads, cache_k, preferred_element_type=jnp.float32)
        * scale
    )
    fresh_scores = (
        jnp.einsum("psgqd,ptgd->pgqst", query_heads, fresh_k, preferred_element_type=jnp.float32)
        * scale
    )
    slots = jnp.arange(suffix_len, dtype=jnp.int32)
    used = slots[None, :] < lengths[:, None]
    suffix_scores = jnp.where(used[:, None, None, None, :], suffix_scores, -jnp.inf)
    step_ids = jnp.arange(steps, dtype=jnp.int32)
    causal = step_ids[None, :] <= step_ids[:, None]
    fresh_scores = jnp.where(causal, fresh_scores, -jnp.inf)
    scores = jnp.concatenate([prompt_scores, suffix_scores, fresh_scores], axis=-1)
    top = jnp.max(scores, axis=-1, keepdims=True)
    expo = jnp.exp(scores - top)
    weights = (expo / jnp.sum(expo, axis=-1, keepdims=True)).astype(jnp.bfloat16)
    w_prompt = weights[..., :prompt_len]
    w_suffix = weights[..., prompt_len : prompt_len + suffix_len]
    w_fresh = weights[..., prompt_len + suffix_len :]

    def mix_one(weight_block):
        return jnp.einsum(
            "gqst,tgd->sgqd", weight_block, prompt_v, preferred_element_type=jnp.float32
        )

    prompt_part = lax.map(mix_one, w_prompt)
    suffix_part = jnp.einsum(
        "pgqsj,pjgd->psgqd", w_suffix, cache_v, preferred_element_type=jnp.float32
    )
    fresh_part = jnp.einsum(
        "pgqst,ptgd->psgqd", w_fresh, fresh_v, preferred_element_type=jnp.float32
    )
    attended = (
        (prompt_part + suffix_part + fresh_part)
        .astype(jnp.bfloat16)
        .reshape(part_rows * steps, q_cols)
    )
    width_share = out_weight.shape[1] // lax.axis_size("tp")
    summed = lax.psum_scatter(
        lax.dot_general(
            out_weight, attended, (((0,), (1,)), ((), ())), preferred_element_type=jnp.float32
        ).astype(jnp.bfloat16),
        "tp",
        scatter_dimension=0,
        tiled=True,
    ).astype(jnp.float32)
    mixed = summed.T.astype(jnp.bfloat16).reshape(part_rows, steps, width_share)
    fresh = jnp.stack((new_keys, new_values), axis=1)
    cache = suffix_cache
    for step in range(steps):
        chosen = slots[None, :] == lengths[:, None] + step
        cache = jnp.where(chosen[:, None, :, None], fresh[:, :, step][:, :, None, :], cache)
    live = slots[None, :] < lengths[:, None] + steps
    cache = jnp.where(live[:, None, :, None], cache, jnp.zeros((), jnp.bfloat16))
    extended = padded(cache, (("dom", 0),), part_rows)
    first_row = lax.axis_index("dom") * part_rows - part_rows
    local_rows = ancestors - first_row
    new_cache = jnp.take(extended, local_rows, axis=0)
    return (mixed, new_cache)


def solution(mesh):
    in_specs = (
        P("dom", None, "tp"),
        P("dom", None, "tp"),
        P("dom", None, "tp"),
        P(None, "tp"),
        P(None, "tp"),
        P("dom", None, None, "tp"),
        P("dom"),
        P("dom"),
        P("tp", None),
    )
    out_specs = (P("dom", None, "tp"), P("dom", None, None, "tp"))
    return jax.shard_map(body, mesh=mesh, in_specs=in_specs, out_specs=out_specs, check_vma=False)
```

profile of v0, /device:TPU:6, one launch (start us, length us, event | category | flops | bytes accessed | tf_op | source)
XLA Modules:
  0.0 134.1 jit_solution(9662467350378453530)
XLA Ops:
  9.6 5.8 %select_select_fusion = bf16[16,2,256,128]{3,2,1,0:T(8,128)(2,1)} fusion(bf16[16,2,256,128]{3,2,1,0:T(8,128)(2,1)} %param.18, pred[16,256]{1,0:T(8,128)(4,1)S(1)} %get-tuple-element.84, pred[16,256]{1,0:T(8,128)(4,1)S(1)} %get-tuple-element.90, pred[16,256]{1,0:T(8,128)(4,1)S(1)} %get-tuple-element.91, pred[16,256]{1,0:T(8,128)(4,1)S(1)} %get-tuple-element.92, ...), kind=kLoop, calls=%fused_computation.22 | loop fusion | flops 5242880 | bytes 4247552 | tf_op jit(solution)/shard_map/jit(_where)/select_n | solution.py:112
  15.4 3.8 %collective-permute-start = (bf16[16,2,256,128]{3,2,1,0:T(8,128)(2,1)}, bf16[16,2,256,128]{3,2,1,0:T(8,128)(2,1)}, u32[]{:S(2)}, u32[]{:S(2)}) collective-permute-start(bf16[16,2,256,128]{3,2,1,0:T(8,128)(2,1)} %select_select_fusion), channel_id=1, source_target_pairs={{0,8},{8,16},{16,24},{24,32},{32,40},{40,48},{48,56},{56,64},{64,7... | collective-permute-start | bytes 6291464 | tf_op jit(solution)/shard_map/ppermute | solution.py:18
  19.2 6.1 %collective-permute-start.1 = (bf16[16,2,256,128]{3,2,1,0:T(8,128)(2,1)}, bf16[16,2,256,128]{3,2,1,0:T(8,128)(2,1)}, u32[]{:S(2)}, u32[]{:S(2)}) collective-permute-start(bf16[16,2,256,128]{3,2,1,0:T(8,128)(2,1)} %select_select_fusion), channel_id=1, source_target_pairs={{8,0},{16,8},{24,16},{32,24},{40,32},{48,40},{56,48},{64,56},{72,6... | collective-permute-start | bytes 6291464 | tf_op jit(solution)/shard_map/ppermute | solution.py:19
  25.5 15.7 %while.20 = (s32[]{:T(128)}, f32[16,1,8,4,2048]{4,2,3,1,0:T(8,128)}, bf16[16,4,1,8,128]{4,3,1,2,0:T(8,128)(2,1)S(1)}, bf16[2048,1,128]{2,0,1:T(8,128)(2,1)S(1)}, s32[]{:T(128)}) while((s32[]{:T(128)}, f32[16,1,8,4,2048]{4,2,3,1,0:T(8,128)}, bf16[16,4,1,8,128]{4,3,1,2,0:T(8,128)(2,1)S(1)}, bf16[2048,1,128]{2,0,1:T(8,128)(2,1)S(1)}, ...), condition=%wide.region_1.2_spmd, body=%wide.region_0.1_spmd.sunk | while | flops 16777216 | bytes 795709 | solution.py:55
  41.2 4.7 %fusion.36 = (f32[16,8,4]{1,2,0:T(4,128)S(1)}, f32[16,1,8,4,2048]{4,2,3,0,1:T(8,128)}) fusion(f32[16,1,8,4,2048]{4,2,3,1,0:T(8,128)} %get-tuple-element.46), kind=kLoop, calls=%fused_computation.77 | loop fusion | flops 2096640 | bytes 8390656 | tf_op jit(solution)/shard_map/reduce_max | solution.py:72
  47.7 2.9 %fusion.12 = f32[16,8,4]{1,2,0:T(4,128)S(1)} fusion(f32[16,1,8,4,4]{4,2,3,0,1:T(8,128)S(1)} %copy.24, f32[16,1,8,4,256]{4,2,3,0,1:T(8,128)S(1)} %get-tuple-element.89, f32[16,1,8,4,2048]{4,2,3,0,1:T(8,128)} %get-tuple-element.75, f32[16,8,4]{1,2,0:T(4,128)S(1)} %bitcast.155), kind=kLoop, calls=%fused_computation.20 | loop fusion | flops 4726272 | bytes 4730880 | tf_op jit(solution)/shard_map/reduce_sum | solution.py:74
  51.1 2.1 %divide_convert_fusion = bf16[16,1,8,4,2308]{4,2,3,0,1:T(8,128)(2,1)S(1)} fusion(f32[16,1,8,4,4]{4,2,3,0,1:T(8,128)S(1)} %copy.24, f32[16,1,8,4,256]{4,2,3,0,1:T(8,128)} %copy-done.4, f32[16,1,8,4,2048]{4,2,3,0,1:T(8,128)S(1)} %copy-done, f32[16,8,4]{1,2,0:T(4,128)S(1)} %fusion.12, f32[16,8,4]{1,2,0:T(4,128)S(1)} %bitcast.156), kind=kLoop, calls=%fused_computation.16 | loop fusion | flops 5908480 | bytes 7094272 | tf_op jit(solution)/shard_map/convert_element_type | solution.py:74
  53.2 1.6 %slice_bitcast_fusion = bf16[16,1,8,4,2048]{4,2,3,1,0:T(8,128)(2,1)} fusion(bf16[16,1,8,4,2308]{4,2,3,0,1:T(8,128)(2,1)S(1)} %divide_convert_fusion), kind=kLoop, calls=%fused_computation.21 | loop fusion | bytes 4194304 | tf_op jit(solution)/shard_map/while | solution.py:84
  54.8 18.0 %while.21 = (s32[]{:T(128)}, f32[16,4,1,8,128]{4,3,1,2,0:T(8,128)S(1)}, bf16[16,1,8,4,2048]{4,2,3,1,0:T(8,128)(2,1)}, bf16[2048,1,128]{2,0,1:T(8,128)(2,1)S(1)}, s32[]{:T(128)}) while((s32[]{:T(128)}, f32[16,4,1,8,128]{4,3,1,2,0:T(8,128)S(1)}, bf16[16,1,8,4,2048]{4,2,3,1,0:T(8,128)(2,1)}, bf16[2048,1,128]{2,0,1:T(8,128)(2,1)S(1)}, ...), condition=%wide.region_7.8_spmd, body=%wide.region_6.7_spmd.sunk | while | flops 16777216 | bytes 672829 | solution.py:84
  55.9 1.1 fusion.53
  57.0 1.1 fusion.53
  58.2 1.1 fusion.53
  59.3 1.1 fusion.53
  60.4 1.1 fusion.53
  61.5 1.1 fusion.53
  62.7 1.1 fusion.53
  63.8 1.1 fusion.53
  73.0 1.5 %fusion.18 = bf16[16,4,1,8,128]{4,3,1,0,2:T(8,128)(2,1)S(1)} fusion(f32[16,4,1,8,128]{4,3,1,0,2:T(8,128)S(1)} %convolution_bitcast_fusion.2, bf16[16,2,256,128]{3,2,1,0:T(8,128)(2,1)} %param.18, bf16[16,1,8,4,2308]{4,2,3,0,1:T(8,128)(2,1)S(1)} %divide_convert_fusion, f32[16,4,1,8,128]{4,3,1,2,0:T(8,128)S(1)} %get-tuple-element.47), kind=kOutput, calls=%fused_computation.32 | convolution fusion | flops 33751040 | bytes 1966080 | tf_op jit(solution)/shard_map/pgqsj,pjgd->psgqd/dot_general | solution.py:85
  74.5 5.8 %fusion.11 = bf16[4096,64]{0,1:T(8,128)(2,1)} fusion(bf16[1024,4096]{1,0:T(8,128)(2,1)} %param.21, bf16[8,8,8,128]{3,2,1,0:T(8,128)(2,1)S(1)} %bitcast.154), kind=kOutput, calls=%fused_computation.18 | convolution fusion | flops 537133056 | bytes 9043968 | tf_op jit(solution)/shard_map/dot_general | solution.py:98
  80.3 33.6 %reduce-scatter.2.cloned.1.call-done = bf16[512,64]{0,1:T(8,128)(2,1)} async-done(((bf16[4096,64]{0,1:T(8,128)(2,1)}), bf16[512,64]{0,1:T(8,128)(2,1)}) %reduce-scatter.2.cloned.1.call-update) | async-done | bytes 65552 | tf_op jit(solution)/shard_map/reduce_scatter | solution.py:97
  113.9 1.5 %reshape.306 = bf16[16,4,512]{2,1,0:T(4,128)(2,1)} reshape(bf16[64,512]{1,0:T(8,128)(2,1)} %bitcast.158) | data formatting | bytes 131072 | tf_op jit(solution)/shard_map/reshape | solution.py:105
  115.4 6.5 %pad_maximum_fusion = bf16[48,2,256,128]{3,2,1,0:T(8,128)(2,1)} fusion(bf16[16,2,256,128]{3,2,1,0:T(8,128)(2,1)} %collective-permute-done.1, bf16[16,2,256,128]{3,2,1,0:T(8,128)(2,1)} %select_select_fusion, bf16[16,2,256,128]{3,2,1,0:T(8,128)(2,1)} %collective-permute-done), kind=kLoop, calls=%fused_computation.13 | loop fusion | flops 6291456 | bytes 12582912 | tf_op jit(solution)/shard_map/concatenate | solution.py:20
  121.9 3.7 %gather_fusion = bf16[16,2,256,128]{3,2,1,0:T(8,128)(2,1)S(1)} fusion(bf16[48,2,256,128]{3,2,1,0:T(8,128)(2,1)} %pad_maximum_fusion, s32[1024]{0:T(1024)S(1)} %pad_clamp_fusion), kind=kCustom, calls=%fused_computation | custom fusion | bytes 4194368 | tf_op jit(solution)/shard_map/jit(_take)/gather | solution.py:116
  125.6 1.6 %broadcast_select_fusion = bf16[16,2,256,128]{3,2,1,0:T(8,128)(2,1)} fusion(bf16[16,2,256,128]{3,2,1,0:T(8,128)(2,1)S(1)} %gather_fusion, pred[16]{0:T(512)(128)(4,1)S(1)} %get-tuple-element.72), kind=kLoop, calls=%fused_computation.23 | loop fusion | flops 1048576 | bytes 4194320 | tf_op jit(solution)/shard_map/jit(_take)/select_n | solution.py:116
  (68 shorter events, 29.5 us)
Async XLA Ops:
  7.2 18.2 %copy-start.5 = (bf16[16,4,1024]{2,1,0:T(4,128)(2,1)S(1)}, bf16[16,4,1024]{2,1,0:T(4,128)(2,1)}, u32[]{:S(2)}) copy-start(bf16[16,4,1024]{2,1,0:T(4,128)(2,1)} %param.13) | copy-start | bytes 393220
  7.2 18.4 %copy-start.1 = (bf16[2048,128]{1,0:T(8,128)(2,1)S(1)}, bf16[2048,128]{1,0:T(8,128)(2,1)}, u32[]{:S(2)}) copy-start(bf16[2048,128]{1,0:T(8,128)(2,1)} %param.16) | copy-start | bytes 1572868
  7.2 106.7 %reduce-scatter.2.cloned.1.call-start = ((), (), s32[]{:S(2)}) async-start(), calls=%async_computation.1 | async-start | bytes 589824 | tf_op jit(solution)/shard_map/reduce_scatter | solution.py:97
  15.4 100.0 %collective-permute-start = (bf16[16,2,256,128]{3,2,1,0:T(8,128)(2,1)}, bf16[16,2,256,128]{3,2,1,0:T(8,128)(2,1)}, u32[]{:S(2)}, u32[]{:S(2)}) collective-permute-start(bf16[16,2,256,128]{3,2,1,0:T(8,128)(2,1)} %select_select_fusion), channel_id=1, source_target_pairs={{0,8},{8,16},{16,24},{24,32},{32,40},{40,48},{48,56},{56,64},{64,7... | collective-permute-start | bytes 6291464 | tf_op jit(solution)/shard_map/ppermute | solution.py:18
  19.2 96.2 %collective-permute-start.1 = (bf16[16,2,256,128]{3,2,1,0:T(8,128)(2,1)}, bf16[16,2,256,128]{3,2,1,0:T(8,128)(2,1)}, u32[]{:S(2)}, u32[]{:S(2)}) collective-permute-start(bf16[16,2,256,128]{3,2,1,0:T(8,128)(2,1)} %select_select_fusion), channel_id=1, source_target_pairs={{8,0},{16,8},{24,16},{32,24},{40,32},{48,40},{56,48},{64,56},{72,6... | collective-permute-start | bytes 6291464 | tf_op jit(solution)/shard_map/ppermute | solution.py:19
  41.2 4.7 %copy-start.3 = (bf16[16,2,256,128]{3,2,1,0:T(8,128)(2,1)S(1)}, bf16[16,2,256,128]{3,2,1,0:T(8,128)(2,1)}, u32[]{:S(2)}) copy-start(bf16[16,2,256,128]{3,2,1,0:T(8,128)(2,1)} %param.18) | copy-start | bytes 6291460
  41.2 5.2 %copy-start.7 = (bf16[16,4,128]{2,1,0:T(4,128)(2,1)S(1)}, bf16[16,4,128]{2,1,0:T(4,128)(2,1)}, u32[]{:S(2)}) copy-start(bf16[16,4,128]{2,1,0:T(4,128)(2,1)} %param.14) | copy-start | bytes 49156
  46.5 1.2 copy-start.4
  47.6 3.5 %copy-start = (f32[16,1,8,4,2048]{4,2,3,0,1:T(8,128)S(1)}, f32[16,1,8,4,2048]{4,2,3,0,1:T(8,128)}, u32[]{:S(2)}) copy-start(f32[16,1,8,4,2048]{4,2,3,0,1:T(8,128)} %get-tuple-element.75) | copy-start | bytes 12582916
  51.1 3.7 %copy-start.2 = (bf16[2048,128]{1,0:T(8,128)(2,1)S(1)}, bf16[2048,128]{1,0:T(8,128)(2,1)}, u32[]{:S(2)}) copy-start(bf16[2048,128]{1,0:T(8,128)(2,1)} %param.17) | copy-start | bytes 1572868
  53.2 19.6 %copy-start.6 = (bf16[16,4,128]{2,1,0:T(4,128)(2,1)S(1)}, bf16[16,4,128]{2,1,0:T(4,128)(2,1)}, u32[]{:S(2)}) copy-start(bf16[16,4,128]{2,1,0:T(4,128)(2,1)} %param.15) | copy-start | bytes 49156
  74.5 5.8 %copy-start.8 = (s32[16]{0:T(128)S(1)}, s32[16]{0:T(128)}, u32[]{:S(2)}) copy-start(s32[16]{0:T(128)} %param.20) | copy-start | bytes 196
Sparse Core Ops, SparseCore 0:
  80.4 33.4 reduce-scatter.1
where the time goes:
time: 135 us; the launch traced here: 134 us
  matrix products  42 us (31%)
  waiting for transfers between devices  33.6 us (25%)
  other arithmetic  25.1 us (19%)
  between operations  14.3 us (11%)
  starting transfers between devices  9.98 us (7%)
  local copies, waits for them, and re-layouts  8.76 us (6%)
    reduce_scatter x1, waiting for transfers between devices, body(): lax.psum_scatter(lax.dot_general(out_weight, attended, (((0,), (1,)), (()...  33.6 us
    dot_general x16, matrix products, mix_one(): jnp.einsum('gqst,tgd->sgqd', weight_block, prompt_v, preferred_element_ty...  17.7 us
    dot_general x16, matrix products, score_one(): jnp.einsum('sgqd,tgd->gqst', query_block, prompt_k, preferred_element_typ...  15.7 us
    concatenate x1, other arithmetic, padded(): value = jnp.concatenate([before, value, after], axis=dim)  6.48 us
    ppermute x1, starting transfers between devices, padded(): after = lax.ppermute(leading, axis, down)  6.13 us
    select_n x1, other arithmetic, body(): jnp.where(live[:, None, :, None], cache, jnp.zeros((), jnp.bfloat16))  5.76 us
    dot_general x1, matrix products, body(): lax.dot_general(out_weight, attended, (((0,), (1,)), ((), ())), preferred...  5.75 us
    reduce_max x2, other arithmetic, body(): top = jnp.max(scores, axis=-1, keepdims=True)  4.69 us
  transfers between devices with their start and end apart: 3, of which 1 were waited for; matrix products, arithmetic and copies ran while one was open for 41% of the time, Pallas kernels for 0%

commit v1 on v0

v1 whole, which is shorter than its diff:
```python
import functools
import math

import jax
import jax.numpy as jnp
from jax import lax
from jax.experimental import pallas as pl
from jax.experimental.pallas import tpu as pltpu
from jax.sharding import PartitionSpec as P

HD = 128
TILE = 16
F32 = jnp.float32
BF16 = jnp.bfloat16


def params(mib):
    return pltpu.CompilerParams(vmem_limit_bytes=mib * 1024 * 1024)


VMEM = pl.BlockSpec(memory_space=pltpu.VMEM)
SMEM = pl.BlockSpec(memory_space=pltpu.SMEM)
ANY = pl.BlockSpec(memory_space=pl.ANY)


def append_kernel(
    len_ref, anc_ref, cache_ref, nk_ref, nv_ref, app_ref, out_ref, in_sems, out_sems
):
    rows, _, slots, hd = app_ref.shape
    steps = nk_ref.shape[1]
    first = lax.axis_index("dom") * rows
    for p in range(rows):
        pltpu.make_async_copy(cache_ref.at[p], app_ref.at[p], in_sems.at[p]).start()
    span = 2 * TILE
    iota = lax.broadcasted_iota(jnp.int32, (span, hd), 0)
    for p in range(rows):
        pltpu.make_async_copy(cache_ref.at[p], app_ref.at[p], in_sems.at[p]).wait()
        length = len_ref[p]
        base = pl.multiple_of(jnp.minimum(length // TILE * TILE, slots - span), TILE)
        at = iota + (base - length)
        for kv, fresh_ref in ((0, nk_ref), (1, nv_ref)):
            fresh = fresh_ref[p].astype(F32)
            win = app_ref[p, kv, pl.ds(base, span), :].astype(F32)
            for t in range(steps):
                win = jnp.where(at == t, fresh[t : t + 1], win)
            win = jnp.where(at >= steps, 0.0, win)
            app_ref[p, kv, pl.ds(base, span), :] = win.astype(BF16)

        def clear(j, carry):
            row = pl.multiple_of(j * TILE, TILE)
            app_ref[p, :, pl.ds(row, TILE), :] = jnp.zeros((2, TILE, hd), BF16)
            return carry

        lax.fori_loop((base + span) // TILE, slots // TILE, clear, 0)
    for c in range(rows):
        local = anc_ref[c] - first

        @pl.when(jnp.logical_and(local >= 0, local < rows))
        def _():
            pltpu.make_async_copy(app_ref.at[local], out_ref.at[c], out_sems.at[c]).start()

    for c in range(rows):
        local = anc_ref[c] - first

        @pl.when(jnp.logical_and(local >= 0, local < rows))
        def _():
            pltpu.make_async_copy(app_ref.at[local], out_ref.at[c], out_sems.at[c]).wait()


def append(lengths, ancestors, cache, new_keys, new_values):
    rows = cache.shape[0]
    return pl.pallas_call(
        append_kernel,
        out_shape=(
            jax.ShapeDtypeStruct(cache.shape, BF16),
            jax.ShapeDtypeStruct(cache.shape, BF16),
        ),
        in_specs=[SMEM, SMEM, ANY, VMEM, VMEM],
        out_specs=(VMEM, ANY),
        scratch_shapes=[pltpu.SemaphoreType.DMA((rows,)), pltpu.SemaphoreType.DMA((rows,))],
        compiler_params=params(8),
        name="append",
    )(lengths, ancestors, cache, new_keys, new_values)


def attend_kernel(
    len_ref, q_ref, pk_ref, pv_ref, app_ref, w_ref, theirs_ref, ours_ref, qs, att, wbuf, sems
):
    rows, steps, _ = q_ref.shape
    heads = q_ref.shape[2] // HD
    slots = app_ref.shape[2]
    chips, tokens, width = theirs_ref.shape
    core = lax.rem(lax.axis_index("tp"), 2)

    def w_copy(k):
        who = 1 - core if k < chips else core
        block = 2 * (k % chips) + who
        cols = pl.ds(pl.multiple_of(block * width, width), width)
        return pltpu.make_async_copy(w_ref.at[:, cols], wbuf.at[k], sems.at[k])

    for k in range(2 * chips):
        w_copy(k).start()

    pair = 2 * steps
    groups = rows // 2
    block = heads * pair
    for g in range(groups):
        two = jnp.concatenate([q_ref[2 * g].astype(F32), q_ref[2 * g + 1].astype(F32)], 0)
        for h in range(heads):
            qs[pl.ds((g * heads + h) * pair, pair), :] = two[:, h * HD : (h + 1) * HD]

    factor = math.log2(math.e) / math.sqrt(HD)
    per = 2
    big = per * block
    prompt_k = pk_ref[...]
    prompt_v = pv_ref[...]
    r = lax.broadcasted_iota(jnp.int32, (pair, 2 * slots), 0)
    c = lax.broadcasted_iota(jnp.int32, (pair, 2 * slots), 1)
    same = (r // steps) == (c // slots)
    lead = lax.rem(c, slots) - lax.rem(r, steps)
    first = c < slots
    nt = (((1,), (1,)), ((), ()))
    for ch in range(groups // per):
        q = qs[pl.ds(ch * big, big), :].astype(BF16)
        s_prompt = lax.dot_general(q, prompt_k, nt, preferred_element_type=F32)
        s_own = []
        for i in range(per):
            g = ch * per + i
            keys = app_ref[2 * g : 2 * g + 2, 0].reshape(2 * slots, HD)
            s = lax.dot_general(
                q[i * block : (i + 1) * block], keys, nt, preferred_element_type=F32
            )
            limit = jnp.where(first, len_ref[2 * g], len_ref[2 * g + 1])
            seen = jnp.logical_and(same, lead <= limit)
            s = s.reshape(heads, pair, 2 * slots)
            s_own.append(jnp.where(seen[None], s, -1e30).reshape(block, 2 * slots))
        s_own = jnp.concatenate(s_own, 0)
        top = jnp.maximum(
            jnp.max(s_prompt, axis=1, keepdims=True), jnp.max(s_own, axis=1, keepdims=True)
        )
        e_prompt = jnp.exp2((s_prompt - top) * factor)
        e_own = jnp.exp2((s_own - top) * factor)
        total = jnp.sum(e_prompt, axis=1, keepdims=True) + jnp.sum(e_own, axis=1, keepdims=True)
        o = jnp.dot(e_prompt.astype(BF16), prompt_v, preferred_element_type=F32)
        e_own = e_own.astype(BF16)
        own = []
        for i in range(per):
            g = ch * per + i
            values = app_ref[2 * g : 2 * g + 2, 1].reshape(2 * slots, HD)
            own.append(
                jnp.dot(
                    e_own[i * block : (i + 1) * block], values, preferred_element_type=F32
                )
            )
        o = (o + jnp.concatenate(own, 0)) / total
        for i in range(per):
            g = ch * per + i
            for h in range(heads):
                at = i * block + h * pair
                att[pl.ds(g * pair, pair), h * HD : (h + 1) * HD] = o[at : at + pair]

    attended = att[...].astype(BF16)
    for k in range(2 * chips):
        w_copy(k).wait()
        part = jnp.dot(attended, wbuf[k], preferred_element_type=F32)
        if k < chips:
            theirs_ref[k] = part.astype(BF16)
        else:
            ours_ref[k - chips] = part


def attend(lengths, queries, prompt_keys, prompt_values, app, out_weight, chips, width):
    rows, steps, q_cols = queries.shape
    tokens = rows * steps
    flops = 2 * 2 * tokens * q_cols * prompt_keys.shape[0] + 2 * tokens * out_weight.size
    return pl.pallas_call(
        attend_kernel,
        out_shape=(
            jax.ShapeDtypeStruct((chips, tokens, width), BF16),
            jax.ShapeDtypeStruct((chips, tokens, width), F32),
        ),
        in_specs=[SMEM, VMEM, VMEM, VMEM, VMEM, ANY],
        out_specs=(VMEM, VMEM),
        scratch_shapes=[
            pltpu.VMEM((tokens * q_cols // HD, HD), F32),
            pltpu.VMEM((tokens, q_cols), F32),
            pltpu.VMEM((2 * chips, out_weight.shape[0], width), BF16),
            pltpu.SemaphoreType.DMA((2 * chips,)),
        ],
        compiler_params=params(28),
        cost_estimate=pl.CostEstimate(
            flops=flops, bytes_accessed=2 * out_weight.size, transcendentals=0
        ),
        name="attend",
    )(lengths, queries, prompt_keys, prompt_values, app, out_weight)


def pair_sum_kernel(ours_ref, got_ref, keep_ref, *send_refs):
    chips = ours_ref.shape[0]
    me = lax.axis_index("tp") // 2
    for k in range(chips):
        at = lax.rem(me + k, chips)
        both = ours_ref[at] + got_ref[at].astype(F32)
        if k == 0:
            keep_ref[...] = both
        else:
            send_refs[k - 1][...] = both.astype(BF16)


def pair_sum(ours, got):
    chips, tokens, width = ours.shape
    return pl.pallas_call(
        pair_sum_kernel,
        out_shape=(jax.ShapeDtypeStruct((tokens, width), F32),)
        + (jax.ShapeDtypeStruct((tokens, width), BF16),) * (chips - 1),
        in_specs=[VMEM, VMEM],
        out_specs=(VMEM,) * chips,
        compiler_params=params(4),
        name="pair_sum",
    )(ours, got)


def chip_sum_kernel(keep_ref, *refs):
    got_refs, out_ref = refs[:-1], refs[-1]
    rows, steps, _ = out_ref.shape
    total = keep_ref[...]
    for ref in got_refs:
        total = total + ref[...].astype(F32)
    total = total.astype(BF16)
    for p in range(rows):
        out_ref[p] = total[p * steps : (p + 1) * steps]


def chip_sum(keep, got, rows):
    tokens, width = keep.shape
    return pl.pallas_call(
        chip_sum_kernel,
        out_shape=jax.ShapeDtypeStruct((rows, tokens // rows, width), BF16),
        in_specs=[VMEM] * (1 + len(got)),
        out_specs=VMEM,
        compiler_params=params(2),
        name="chip_sum",
    )(keep, *got)


def place_kernel(anc_ref, a_ref, b_ref, held_ref, out_ref, sems):
    del held_ref
    rows = out_ref.shape[0]
    half = a_ref.shape[0]
    me = lax.axis_index("dom")
    even = lax.rem(me, 2) == 0

    def each(act):
        for c in range(rows):
            local = anc_ref[c] - me * rows
            above = local >= rows
            below = local < 0
            up = jnp.logical_and(above, even) | jnp.logical_and(below, jnp.logical_not(even))
            down = jnp.logical_and(below, even) | jnp.logical_and(above, jnp.logical_not(even))
            at = jnp.where(above, local - rows, local + half)
            at = jnp.clip(at, 0, half - 1)

            @pl.when(up)
            def _():
                act(pltpu.make_async_copy(a_ref.at[at], out_ref.at[c], sems.at[c]))

            @pl.when(down)
            def _():
                act(pltpu.make_async_copy(b_ref.at[at], out_ref.at[c], sems.at[c]))

    each(lambda copy: copy.start())
    each(lambda copy: copy.wait())


def place(ancestors, a, b, held):
    rows = held.shape[0]
    return pl.pallas_call(
        place_kernel,
        out_shape=jax.ShapeDtypeStruct(held.shape, BF16),
        in_specs=[SMEM, ANY, ANY, ANY],
        out_specs=ANY,
        scratch_shapes=[pltpu.SemaphoreType.DMA((rows,))],
        input_output_aliases={3: 0},
        compiler_params=params(1),
        name="place",
    )(ancestors, a, b, held)


def body(
    queries,
    new_keys,
    new_values,
    prompt_keys,
    prompt_values,
    suffix_cache,
    lengths,
    ancestors,
    out_weight,
):
    rows, steps, _ = queries.shape
    doms = lax.axis_size("dom")
    tps = lax.axis_size("tp")
    chips = tps // 2
    width = out_weight.shape[1] // tps
    half = rows // 2

    app, held = append(lengths, ancestors, suffix_cache, new_keys, new_values)
    even = lax.rem(lax.axis_index("dom"), 2) == 0
    low, high = app[:half], app[half:]
    pairs_a = [(i, i ^ 1) for i in range(doms)]
    pairs_b = [(i, i + 1) for i in range(1, doms - 1, 2)]
    pairs_b = pairs_b + [(j, i) for i, j in pairs_b]
    to_a = lax.dynamic_slice_in_dim(app, jnp.where(even, half, 0), half, 0)
    to_b = lax.dynamic_slice_in_dim(app, jnp.where(even, 0, half), half, 0)
    from_a = lax.ppermute(to_a, "dom", pairs_a)
    from_b = lax.ppermute(to_b, "dom", pairs_b)

    theirs, ours = attend(
        lengths, queries, prompt_keys, prompt_values, app, out_weight, chips, width
    )
    got = lax.ppermute(theirs, "tp", [(i, i ^ 1) for i in range(tps)])
    keep, *send = pair_sum(ours, got)
    arrived = [
        lax.ppermute(value, "tp", [(i, (i + 2 * k) % tps) for i in range(tps)])
        for k, value in enumerate(send, 1)
    ]
    mixed = chip_sum(keep, arrived, rows)
    new_cache = place(ancestors, from_a, from_b, held)
    return (mixed, new_cache)


def solution(mesh):
    in_specs = (
        P("dom", None, "tp"),
        P("dom", None, "tp"),
        P("dom", None, "tp"),
        P(None, "tp"),
        P(None, "tp"),
        P("dom", None, None, "tp"),
        P("dom"),
        P("dom"),
        P("tp", None),
    )
    out_specs = (P("dom", None, "tp"), P("dom", None, None, "tp"))
    return jax.shard_map(body, mesh=mesh, in_specs=in_specs, out_specs=out_specs, check_vma=False)
```

time: 135 us -> 44.6 us (0.33)
  matrix products: 42 us -> 0 us
  waiting for transfers between devices: 33.6 us -> 5.84 us
  other arithmetic: 25.1 us -> 0 us
  Pallas kernels: 0 us -> 14.6 us
  between operations: 14.3 us -> 0.78 us
  starting transfers between devices: 9.98 us -> 15.2 us
    dot_general x37 -> x0, matrix products: 42 us -> none  [the longest x16 17.7 us: mix_one(): jnp.einsum('gqst,tgd->sgqd', weight_block, prompt_v, preferred_element_ty...]
    reduce_scatter x1 -> x0, waiting for transfers between devices: 33.6 us -> none  [body(): lax.psum_scatter(lax.dot_general(out_weight, attended, (((0,), (1,)), (()...]
    pallas_call x0 -> x5, Pallas kernels: none -> 14.6 us  [the longest x1 6.85 us: attend(): pl.pallas_call(attend_kernel, out_shape=(jax.ShapeDtypeStruct((chips, tok...]
    select_n x2 -> x0, other arithmetic: 7.35 us -> none  [the longest x1 5.76 us: body(): jnp.where(live[:, None, :, None], cache, jnp.zeros((), jnp.bfloat16))]
    unnamed x18 -> x22, local copies, waits for them, and re-layouts: 0.6 us -> 7.73 us
    concatenate x1 -> x0, other arithmetic: 6.48 us -> none  [padded(): value = jnp.concatenate([before, value, after], axis=dim)]
    ppermute x2 -> x6, waiting for transfers between devices: 0.01 us -> 5.84 us  [the longest x3 2.92 us: body(): lax.ppermute(value, 'tp', [(i, (i + 2 * k) % tps) for i in range(tps)])]
    ppermute x2 -> x6, starting transfers between devices: 9.94 us -> 15.2 us  [the longest x1 7.19 us: body(): from_b = lax.ppermute(to_b, 'dom', pairs_b)]
  transfers between devices with their start and end apart: 3 -> 6, of which waited for: 1 -> 4; matrix products, arithmetic and copies ran while one was open for 41% -> 0% of each run, Pallas kernels for 0% -> 17%
where the time goes in v1:
time: 44.6 us; the launch traced here: 44.4 us
  starting transfers between devices  15.2 us (34%)
  Pallas kernels  14.6 us (33%)
  local copies, waits for them, and re-layouts  7.96 us (18%)
  waiting for transfers between devices  5.84 us (13%)
  between operations  0.78 us (2%)
    unnamed x22, local copies, waits for them, and re-layouts  7.73 us
    ppermute x1, starting transfers between devices, body(): from_b = lax.ppermute(to_b, 'dom', pairs_b)  7.19 us
    pallas_call x1, Pallas kernels, attend(): pl.pallas_call(attend_kernel, out_shape=(jax.ShapeDtypeStruct((chips, tok...  6.85 us
    ppermute x3, starting transfers between devices, body(): lax.ppermute(value, 'tp', [(i, (i + 2 * k) % tps) for i in range(tps)])  5.9 us
    pallas_call x1, Pallas kernels, append(): pl.pallas_call(append_kernel, out_shape=(jax.ShapeDtypeStruct(cache.shape...  5.51 us
    ppermute x3, waiting for transfers between devices, body(): lax.ppermute(value, 'tp', [(i, (i + 2 * k) % tps) for i in range(tps)])  2.92 us
    ppermute x1, starting transfers between devices, body(): from_a = lax.ppermute(to_a, 'dom', pairs_a)  2.03 us
    pallas_call x1, Pallas kernels, place(): pl.pallas_call(place_kernel, out_shape=jax.ShapeDtypeStruct(held.shape, B...  1.53 us
  transfers between devices with their start and end apart: 6, of which 4 were waited for; matrix products, arithmetic and copies ran while one was open for 0% of the time, Pallas kernels for 17%

profile of v1, /device:TPU:6, one launch (start us, length us, event | category | flops | bytes accessed | tf_op | source)
XLA Modules:
  0.0 44.4 jit_solution(13989145807649943421)
XLA Ops:
  0.7 1.6 %copy-done.1 = bf16[16,2,256,128]{3,2,1,0:T(8,128)(2,1)S(1)} copy-done((bf16[16,2,256,128]{3,2,1,0:T(8,128)(2,1)S(1)}, bf16[16,2,256,128]{3,2,1,0:T(8,128)(2,1)}, u32[]{:S(2)}) %copy-start.1) | copy-done | bytes 2097176
  2.2 0.7 %copy-done.5 = bf16[16,4,128]{2,1,0:T(4,128)(2,1)S(1)} copy-done((bf16[16,4,128]{2,1,0:T(4,128)(2,1)S(1)}, bf16[16,4,128]{2,1,0:T(4,128)(2,1)}, u32[]{:S(2)}) %copy-start.5) | copy-done | bytes 16408
  3.0 0.7 %copy-done.6 = bf16[16,4,128]{2,1,0:T(4,128)(2,1)S(1)} copy-done((bf16[16,4,128]{2,1,0:T(4,128)(2,1)S(1)}, bf16[16,4,128]{2,1,0:T(4,128)(2,1)}, u32[]{:S(2)}) %copy-start.6) | copy-done | bytes 16408
  3.7 0.7 %copy-done.7 = s32[16]{0:T(128)S(1)} copy-done((s32[16]{0:T(128)S(1)}, s32[16]{0:T(128)}, u32[]{:S(2)}) %copy-start.7) | copy-done | bytes 88
  4.3 0.7 %copy-done.9 = s32[16]{0:T(128)S(1)} copy-done((s32[16]{0:T(128)S(1)}, s32[16]{0:T(128)}, u32[]{:S(2)}) %copy-start.9) | copy-done | bytes 88
  5.0 5.5 %append.1 = (bf16[16,2,256,128]{3,2,1,0:T(8,128)(2,1)S(1)}, bf16[16,2,256,128]{3,2,1,0:T(8,128)(2,1)}) custom-call(s32[16]{0:T(128)S(1)} %copy-done.7, s32[16]{0:T(128)S(1)} %copy-done.9, bf16[16,2,256,128]{3,2,1,0:T(8,128)(2,1)S(1)} %copy-done.1, bf16[16,4,128]{2,1,0:T(4,128)(2,1)S(1)} %copy-done.5, bf16[16,4,128]{2,1,0:T(4,128)(2,1)S(1)} %copy-done.6), custom_call_target="tpu_custom_call" | custom-call | tf_op jit(solution)/shard_map/append/pallas_call | solution.py:72
  10.5 0.0 copy-start.3
  10.5 0.0 copy-start.4
  10.6 0.2 constant_dynamic-slice_fusion
  10.8 2.0 %collective-permute-start.4 = (bf16[8,2,256,128]{3,2,1,0:T(8,128)(2,1)S(1)}, bf16[8,2,256,128]{3,2,1,0:T(8,128)(2,1)S(1)}, u32[]{:S(2)}, u32[]{:S(2)}) collective-permute-start(bf16[8,2,256,128]{3,2,1,0:T(8,128)(2,1)S(1)} %get-tuple-element.19), channel_id=1, source_target_pairs={{0,8},{8,0},{16,24},{24,16},{32,40},{40,32},{48,56},{56,48},{64,72... | collective-permute-start | bytes 3145736 | tf_op jit(solution)/shard_map/ppermute | solution.py:315
  12.8 7.2 %collective-permute-start.5 = (bf16[8,2,256,128]{3,2,1,0:T(8,128)(2,1)S(1)}, bf16[8,2,256,128]{3,2,1,0:T(8,128)(2,1)S(1)}, u32[]{:S(2)}, u32[]{:S(2)}) collective-permute-start(bf16[8,2,256,128]{3,2,1,0:T(8,128)(2,1)S(1)} %get-tuple-element.18), channel_id=1, source_target_pairs={{8,16},{24,32},{40,48},{56,64},{72,80},{88,96},{104,112},{120,128}... | collective-permute-start | bytes 3145736 | tf_op jit(solution)/shard_map/ppermute | solution.py:316
  20.1 3.4 %copy-done = bf16[1024,4096]{1,0:T(8,128)(2,1)S(1)} copy-done((bf16[1024,4096]{1,0:T(8,128)(2,1)S(1)}, bf16[1024,4096]{1,0:T(8,128)(2,1)}, u32[]{:S(2)}) %copy-start) | copy-done | bytes 8388632
  23.4 6.8 %attend.1 = (bf16[4,64,512]{2,1,0:T(8,128)(2,1)S(1)}, f32[4,64,512]{2,1,0:T(8,128)S(1)}) custom-call(s32[16]{0:T(128)S(1)} %copy-done.8, bf16[16,4,1024]{2,1,0:T(4,128)(2,1)S(1)} %copy-done.4, bf16[2048,128]{1,0:T(8,128)(2,1)S(1)} %copy-done.2, bf16[2048,128]{1,0:T(8,128)(2,1)S(1)} %copy-done.3, bf16[16,2,256,128]{3,2,1,0:T(8,128)(2,1)S(1)} %get-tuple-element.10.app_ref, ...), custom_call_target="tpu_custom_call" | custom-call | flops 1073741824 | bytes 8388608 | tf_op jit(solution)/shard_map/attend/pallas_call | solution.py:176
  30.3 0.1 collective-permute-start
  30.4 1.5 %collective-permute-done.got_ref = bf16[4,64,512]{2,1,0:T(8,128)(2,1)S(1)} collective-permute-done((bf16[4,64,512]{2,1,0:T(8,128)(2,1)S(1)}, bf16[4,64,512]{2,1,0:T(8,128)(2,1)S(1)}, u32[]{:S(2)}, u32[]{:S(2)}) %collective-permute-start) | collective-permute-done | bytes 262176 | tf_op jit(solution)/shard_map/ppermute | solution.py:321
  31.9 0.1 pair_sum.1
  32.0 1.7 %collective-permute-start.1 = (bf16[64,512]{1,0:T(8,128)(2,1)S(1)}, bf16[64,512]{1,0:T(8,128)(2,1)S(1)}, u32[]{:S(2)}, u32[]{:S(2)}) collective-permute-start(bf16[64,512]{1,0:T(8,128)(2,1)S(1)} %get-tuple-element.14), channel_id=1, source_target_pairs={{0,2},{1,3},{2,4},{3,5},{4,6},{5,7},{6,0},{7,1},{8,10},{9,11},{10,... | collective-permute-start | bytes 196616 | tf_op jit(solution)/shard_map/ppermute | solution.py:324
  33.6 2.9 %collective-permute-start.2 = (bf16[64,512]{1,0:T(8,128)(2,1)S(1)}, bf16[64,512]{1,0:T(8,128)(2,1)S(1)}, u32[]{:S(2)}, u32[]{:S(2)}) collective-permute-start(bf16[64,512]{1,0:T(8,128)(2,1)S(1)} %get-tuple-element.15), channel_id=1, source_target_pairs={{0,4},{1,5},{2,6},{3,7},{4,0},{5,1},{6,2},{7,3},{8,12},{9,13},{10,... | collective-permute-start | bytes 196616 | tf_op jit(solution)/shard_map/ppermute | solution.py:324
  36.5 1.3 %collective-permute-start.3 = (bf16[64,512]{1,0:T(8,128)(2,1)S(1)}, bf16[64,512]{1,0:T(8,128)(2,1)S(1)}, u32[]{:S(2)}, u32[]{:S(2)}) collective-permute-start(bf16[64,512]{1,0:T(8,128)(2,1)S(1)} %get-tuple-element.16), channel_id=1, source_target_pairs={{0,6},{1,7},{2,0},{3,1},{4,2},{5,3},{6,4},{7,5},{8,14},{9,15},{10,... | collective-permute-start | bytes 196616 | tf_op jit(solution)/shard_map/ppermute | solution.py:324
  37.9 2.2 %collective-permute-done.2.refs_1_ = bf16[64,512]{1,0:T(8,128)(2,1)S(1)} collective-permute-done((bf16[64,512]{1,0:T(8,128)(2,1)S(1)}, bf16[64,512]{1,0:T(8,128)(2,1)S(1)}, u32[]{:S(2)}, u32[]{:S(2)}) %collective-permute-start.2) | collective-permute-done | bytes 65568 | tf_op jit(solution)/shard_map/ppermute | solution.py:324
  40.1 0.8 %collective-permute-done.3.refs_2_ = bf16[64,512]{1,0:T(8,128)(2,1)S(1)} collective-permute-done((bf16[64,512]{1,0:T(8,128)(2,1)S(1)}, bf16[64,512]{1,0:T(8,128)(2,1)S(1)}, u32[]{:S(2)}, u32[]{:S(2)}) %collective-permute-start.3) | collective-permute-done | bytes 65568 | tf_op jit(solution)/shard_map/ppermute | solution.py:324
  40.8 0.7 %chip_sum.1 = bf16[16,4,512]{2,1,0:T(4,128)(2,1)} custom-call(f32[64,512]{1,0:T(8,128)S(1)} %get-tuple-element.13.keep_ref, bf16[64,512]{1,0:T(8,128)(2,1)S(1)} %collective-permute-done.1.refs_0_, bf16[64,512]{1,0:T(8,128)(2,1)S(1)} %collective-permute-done.2.refs_1_, bf16[64,512]{1,0:T(8,128)(2,1)S(1)} %collective-permute-done.3.refs_2_), custom_call_target="tpu_custom_call" | custom-call | tf_op jit(solution)/shard_map/chip_sum/pallas_call | solution.py:236
  41.5 1.4 %collective-permute-done.5.b_ref = bf16[8,2,256,128]{3,2,1,0:T(8,128)(2,1)S(1)} collective-permute-done((bf16[8,2,256,128]{3,2,1,0:T(8,128)(2,1)S(1)}, bf16[8,2,256,128]{3,2,1,0:T(8,128)(2,1)S(1)}, u32[]{:S(2)}, u32[]{:S(2)}) %collective-permute-start.5) | collective-permute-done | bytes 1048608 | tf_op jit(solution)/shard_map/ppermute | solution.py:316
  42.9 1.5 %place.1 = bf16[16,2,256,128]{3,2,1,0:T(8,128)(2,1)} custom-call(s32[16]{0:T(128)S(1)} %copy-done.10, bf16[8,2,256,128]{3,2,1,0:T(8,128)(2,1)S(1)} %collective-permute-done.4.a_ref, bf16[8,2,256,128]{3,2,1,0:T(8,128)(2,1)S(1)} %collective-permute-done.5.b_ref, bf16[16,2,256,128]{3,2,1,0:T(8,128)(2,1)} %get-tuple-element.17.held_ref), custom_call_target="tpu_custom_call", output_to_operand_aliasing={{}: (3, {})} | custom-call | tf_op jit(solution)/shard_map/place/pallas_call | solution.py:277
  (16 shorter events, 0.0 us)
Async XLA Ops:
  0.6 1.6 %copy-start.1 = (bf16[16,2,256,128]{3,2,1,0:T(8,128)(2,1)S(1)}, bf16[16,2,256,128]{3,2,1,0:T(8,128)(2,1)}, u32[]{:S(2)}) copy-start(bf16[16,2,256,128]{3,2,1,0:T(8,128)(2,1)} %cache_ref.1) | copy-start | bytes 6291460
  2.2 0.7 %copy-start.5 = (bf16[16,4,128]{2,1,0:T(4,128)(2,1)S(1)}, bf16[16,4,128]{2,1,0:T(4,128)(2,1)}, u32[]{:S(2)}) copy-start(bf16[16,4,128]{2,1,0:T(4,128)(2,1)} %nk_ref.1) | copy-start | bytes 49156
  3.0 0.7 %copy-start.6 = (bf16[16,4,128]{2,1,0:T(4,128)(2,1)S(1)}, bf16[16,4,128]{2,1,0:T(4,128)(2,1)}, u32[]{:S(2)}) copy-start(bf16[16,4,128]{2,1,0:T(4,128)(2,1)} %nv_ref.1) | copy-start | bytes 49156
  3.7 0.7 %copy-start.7 = (s32[16]{0:T(128)S(1)}, s32[16]{0:T(128)}, u32[]{:S(2)}) copy-start(s32[16]{0:T(128)} %len_ref.3) | copy-start | bytes 196
  4.3 0.7 %copy-start.9 = (s32[16]{0:T(128)S(1)}, s32[16]{0:T(128)}, u32[]{:S(2)}) copy-start(s32[16]{0:T(128)} %anc_ref.3) | copy-start | bytes 196
  10.5 9.5 %copy-start.2 = (bf16[2048,128]{1,0:T(8,128)(2,1)S(1)}, bf16[2048,128]{1,0:T(8,128)(2,1)}, u32[]{:S(2)}) copy-start(bf16[2048,128]{1,0:T(8,128)(2,1)} %pk_ref.1) | copy-start | bytes 1572868
  10.5 9.5 %copy-start.3 = (bf16[2048,128]{1,0:T(8,128)(2,1)S(1)}, bf16[2048,128]{1,0:T(8,128)(2,1)}, u32[]{:S(2)}) copy-start(bf16[2048,128]{1,0:T(8,128)(2,1)} %pv_ref.1) | copy-start | bytes 1572868
  10.5 9.5 %copy-start.4 = (bf16[16,4,1024]{2,1,0:T(4,128)(2,1)S(1)}, bf16[16,4,1024]{2,1,0:T(4,128)(2,1)}, u32[]{:S(2)}) copy-start(bf16[16,4,1024]{2,1,0:T(4,128)(2,1)} %q_ref.1) | copy-start | bytes 393220
  10.5 9.5 %copy-start.8 = (s32[16]{0:T(128)S(1)}, s32[16]{0:T(128)}, u32[]{:S(2)}) copy-start(s32[16]{0:T(128)} %len_ref.3) | copy-start | bytes 196
  10.8 30.7 %collective-permute-start.4 = (bf16[8,2,256,128]{3,2,1,0:T(8,128)(2,1)S(1)}, bf16[8,2,256,128]{3,2,1,0:T(8,128)(2,1)S(1)}, u32[]{:S(2)}, u32[]{:S(2)}) collective-permute-start(bf16[8,2,256,128]{3,2,1,0:T(8,128)(2,1)S(1)} %get-tuple-element.19), channel_id=1, source_target_pairs={{0,8},{8,0},{16,24},{24,16},{32,40},{40,32},{48,56},{56,48},{64,72... | collective-permute-start | bytes 3145736 | tf_op jit(solution)/shard_map/ppermute | solution.py:315
  12.8 30.1 %collective-permute-start.5 = (bf16[8,2,256,128]{3,2,1,0:T(8,128)(2,1)S(1)}, bf16[8,2,256,128]{3,2,1,0:T(8,128)(2,1)S(1)}, u32[]{:S(2)}, u32[]{:S(2)}) collective-permute-start(bf16[8,2,256,128]{3,2,1,0:T(8,128)(2,1)S(1)} %get-tuple-element.18), channel_id=1, source_target_pairs={{8,16},{24,32},{40,48},{56,64},{72,80},{88,96},{104,112},{120,128}... | collective-permute-start | bytes 3145736 | tf_op jit(solution)/shard_map/ppermute | solution.py:316
  20.1 3.4 %copy-start = (bf16[1024,4096]{1,0:T(8,128)(2,1)S(1)}, bf16[1024,4096]{1,0:T(8,128)(2,1)}, u32[]{:S(2)}) copy-start(bf16[1024,4096]{1,0:T(8,128)(2,1)} %w_ref.1) | copy-start | bytes 25165828
  23.4 19.4 %copy-start.10 = (s32[16]{0:T(128)S(1)}, s32[16]{0:T(128)}, u32[]{:S(2)}) copy-start(s32[16]{0:T(128)} %anc_ref.3) | copy-start | bytes 196
  30.3 1.6 %collective-permute-start = (bf16[4,64,512]{2,1,0:T(8,128)(2,1)S(1)}, bf16[4,64,512]{2,1,0:T(8,128)(2,1)S(1)}, u32[]{:S(2)}, u32[]{:S(2)}) collective-permute-start(bf16[4,64,512]{2,1,0:T(8,128)(2,1)S(1)} %get-tuple-element.12), channel_id=1, source_target_pairs={{0,1},{1,0},{2,3},{3,2},{4,5},{5,4},{6,7},{7,6},{8,9},{9,8},{10,11... | collective-permute-start | bytes 786440 | tf_op jit(solution)/shard_map/ppermute | solution.py:321
  32.0 5.9 %collective-permute-start.1 = (bf16[64,512]{1,0:T(8,128)(2,1)S(1)}, bf16[64,512]{1,0:T(8,128)(2,1)S(1)}, u32[]{:S(2)}, u32[]{:S(2)}) collective-permute-start(bf16[64,512]{1,0:T(8,128)(2,1)S(1)} %get-tuple-element.14), channel_id=1, source_target_pairs={{0,2},{1,3},{2,4},{3,5},{4,6},{5,7},{6,0},{7,1},{8,10},{9,11},{10,... | collective-permute-start | bytes 196616 | tf_op jit(solution)/shard_map/ppermute | solution.py:324
  33.6 6.4 %collective-permute-start.2 = (bf16[64,512]{1,0:T(8,128)(2,1)S(1)}, bf16[64,512]{1,0:T(8,128)(2,1)S(1)}, u32[]{:S(2)}, u32[]{:S(2)}) collective-permute-start(bf16[64,512]{1,0:T(8,128)(2,1)S(1)} %get-tuple-element.15), channel_id=1, source_target_pairs={{0,4},{1,5},{2,6},{3,7},{4,0},{5,1},{6,2},{7,3},{8,12},{9,13},{10,... | collective-permute-start | bytes 196616 | tf_op jit(solution)/shard_map/ppermute | solution.py:324
  36.5 4.3 %collective-permute-start.3 = (bf16[64,512]{1,0:T(8,128)(2,1)S(1)}, bf16[64,512]{1,0:T(8,128)(2,1)S(1)}, u32[]{:S(2)}, u32[]{:S(2)}) collective-permute-start(bf16[64,512]{1,0:T(8,128)(2,1)S(1)} %get-tuple-element.16), channel_id=1, source_target_pairs={{0,6},{1,7},{2,0},{3,1},{4,2},{5,3},{6,4},{7,5},{8,14},{9,15},{10,... | collective-permute-start | bytes 196616 | tf_op jit(solution)/shard_map/ppermute | solution.py:324

commit v2 on v1

v2 whole, which is shorter than its diff:
```python
import functools
import math

import jax
import jax.numpy as jnp
from jax import lax
from jax.experimental import pallas as pl
from jax.experimental.pallas import tpu as pltpu
from jax.sharding import PartitionSpec as P

HD = 128
TILE = 16
HEAD = 109
SLACK = HEAD - 15
F32 = jnp.float32
BF16 = jnp.bfloat16
VMEM = pl.BlockSpec(memory_space=pltpu.VMEM)
SMEM = pl.BlockSpec(memory_space=pltpu.SMEM)
HBM = pl.BlockSpec(memory_space=pltpu.HBM)
ANY = pl.BlockSpec(memory_space=pl.ANY)


def params(mib):
    return pltpu.CompilerParams(vmem_limit_bytes=mib * 1024 * 1024)


def in_hbm(value):
    return pltpu.with_memory_space_constraint(value, pltpu.HBM)


def like(value):
    return jax.ShapeDtypeStruct(value.shape, value.dtype)


def live_tiles(length, steps):
    return (length + steps + TILE - 1) // TILE


def tiles(first, count):
    return pl.ds(pl.multiple_of(first * TILE, TILE), pl.multiple_of(count * TILE, TILE))


def own_base(side, rows):
    even = lax.rem(lax.axis_index("dom"), 2) == 0
    return jnp.where(even, rows // 2 * (1 - side), rows // 2 * side)


def partner_of(side):
    me = lax.axis_index("dom")
    even = lax.rem(me, 2) == 0
    return jnp.where(even, me + 1 - 2 * side, me - 1 + 2 * side)


def assign(lens, base, places, steps):
    used = jnp.int32(1)
    for r in range(places.shape[0]):
        places[r] = used
        used = used + live_tiles(lens[base + r], steps)
    return used


def load_all(sources, targets, sems):
    copies = [
        pltpu.make_async_copy(a, b, sems.at[i]) for i, (a, b) in enumerate(zip(sources, targets))
    ]
    for copy in copies:
        copy.start()
    for copy in copies:
        copy.wait()


def tile_at(tile):
    return pl.ds(pl.multiple_of(tile * TILE, TILE), TILE)


def insert(target, at, tile, length, fresh, steps):
    line = lax.broadcasted_iota(jnp.int32, (TILE, HD), 0) + (tile * TILE - length)
    rows = target[at].astype(F32)
    for t in range(steps):
        rows = jnp.where(line == t, fresh[t : t + 1], rows)
    target[at] = jnp.where(line >= steps, 0.0, rows).astype(BF16)


def first_kernel(
    len_hbm, cache_ref, nk_hbm, nv_hbm, head_a, head_b, tail_a, tail_b,
    lens, nk, nv, place_a, place_b, spare, sems, head_sems, spare_sem,
):
    rows, kinds, slots, hd = cache_ref.shape
    half = rows // 2
    steps = nk.shape[1]
    copies = [
        pltpu.make_async_copy(a, b, sems.at[i])
        for i, (a, b) in enumerate(((len_hbm, lens), (nk_hbm, nk), (nv_hbm, nv)))
    ]
    for copy in copies:
        copy.start()
    copies[0].wait()
    sides = []
    for side, places, head, tail in ((0, place_a, head_a, tail_a), (1, place_b, head_b, tail_b)):
        base = own_base(side, rows)
        sides.append((side, base, assign(lens, base, places, steps), places, head, tail))

    def spots():
        for side, base, _, places, head, _ in sides:
            for r in range(half):
                count = live_tiles(lens[base + r], steps)
                copy = pltpu.make_async_copy(
                    cache_ref.at[base + r, :, tiles(0, count)],
                    head.at[:, tiles(places[r], count)],
                    head_sems.at[side, r],
                )
                yield places[r] + count <= HEAD, copy, base + r, count, places[r], head

    for fits, copy, *_ in spots():

        @pl.when(fits)
        def _():
            copy.start()

    for _, base, used, _, head, _ in sides:
        line = lax.broadcasted_iota(jnp.int32, (TILE, hd), 0)
        words = jnp.where(line == half, (used > HEAD).astype(jnp.int32), 0)
        for r in range(half):
            words = jnp.where(line == r, lens[base + r], words)
        head[0, :TILE, :] = words.astype(F32).astype(BF16)
    for copy in copies[1:]:
        copy.wait()

    def renew(target, place, p, count):
        for kv, fresh_ref in ((0, nk), (1, nv)):
            fresh = fresh_ref[p].astype(F32)
            for tile in (jnp.maximum(count - 2, 0), count - 1):
                insert(target, (kv, tile_at(place + tile)), tile, lens[p], fresh, steps)

    for fits, copy, p, count, place, head in spots():

        @pl.when(fits)
        def _():
            copy.wait()
            renew(head, place, p, count)

    for _, base, used, places, _, tail in sides:

        @pl.when(used > HEAD)
        def _():
            for r in range(half):
                count = live_tiles(lens[base + r], steps)
                place = places[r]

                @pl.when(place + count > HEAD)
                def _():
                    bring = pltpu.make_async_copy(cache_ref.at[base + r], spare, spare_sem.at[0])
                    bring.start()
                    bring.wait()
                    renew(spare, 0, base + r, count)
                    source = spare.at[:, tiles(0, count)]
                    target = tail.at[:, tiles(place - SLACK, count)]
                    leave = pltpu.make_async_copy(source, target, spare_sem.at[0])
                    leave.start()
                    leave.wait()


def first(lengths, cache, new_keys, new_values):
    rows, kinds, slots, hd = cache.shape
    half = rows // 2
    args = (lengths, cache, new_keys, new_values)
    head = jax.ShapeDtypeStruct((kinds, HEAD * TILE, hd), BF16)
    tail = jax.ShapeDtypeStruct((kinds, (half * slots // TILE + 1 - SLACK) * TILE, hd), BF16)
    return pl.pallas_call(
        first_kernel,
        out_shape=(
            head, head, tail, tail,
        ),
        in_specs=[HBM] * len(args),
        out_specs=(VMEM,) * 2 + (HBM,) * 2,
        scratch_shapes=[
            pltpu.SMEM((rows,), jnp.int32),
            pltpu.VMEM(new_keys.shape, BF16),
            pltpu.VMEM(new_values.shape, BF16),
            pltpu.SMEM((half,), jnp.int32),
            pltpu.SMEM((half,), jnp.int32),
            pltpu.VMEM(cache.shape[1:], BF16),
            pltpu.SemaphoreType.DMA((3,)),
            pltpu.SemaphoreType.DMA((2, half)),
            pltpu.SemaphoreType.DMA((1,)),
        ],
        compiler_params=params(4),
        name="first",
    )(*map(in_hbm, args))


def keep_kernel(steps, len_in, anc_in, app_ref, out_ref, lens, ancs, zero, live_sems, zero_sems, sems):
    rows, _, slots, _ = out_ref.shape
    first = lax.axis_index("dom") * rows
    zero[...] = jnp.zeros_like(zero)
    load_all((len_in, anc_in), (lens, ancs), sems)

    def each(act):
        @pl.loop(0, rows)
        def _(child):
            row = ancs[child] - first
            here = jnp.logical_and(row >= 0, row < rows)
            at = jnp.clip(row, 0, rows - 1)
            count = jnp.where(here, live_tiles(lens[at], steps), 0)
            rest = slots // TILE - count

            @pl.when(here)
            def _():
                part = tiles(0, count)
                source = app_ref.at[at, :, part]
                act(pltpu.make_async_copy(source, out_ref.at[child, :, part], live_sems.at[child]))

            @pl.when(rest > 0)
            def _():
                source = zero.at[:, tiles(0, rest)]
                target = out_ref.at[child, :, tiles(count, rest)]
                act(pltpu.make_async_copy(source, target, zero_sems.at[child]))

    each(lambda copy: copy.start())
    each(lambda copy: copy.wait())


def keep(steps, lengths, ancestors, app):
    rows = app.shape[0]
    return pl.pallas_call(
        functools.partial(keep_kernel, steps),
        out_shape=like(app),
        in_specs=[ANY, ANY, VMEM],
        out_specs=HBM,
        scratch_shapes=[
            pltpu.SMEM((rows,), jnp.int32),
            pltpu.SMEM((rows,), jnp.int32),
            pltpu.VMEM(app.shape[1:], BF16),
            pltpu.SemaphoreType.DMA((rows,)),
            pltpu.SemaphoreType.DMA((rows,)),
            pltpu.SemaphoreType.DMA((2,)),
        ],
        compiler_params=params(1),
        name="keep",
    )(lengths, ancestors, app)


def remote_rows(ancs, lens, places, rows, act):
    half = rows // 2
    me = lax.axis_index("dom")
    for side in range(2):
        partner = partner_of(side)
        children = jnp.where(partner > me, half, 0)
        for i in range(half):
            child = children + i
            row = ancs[child] - partner * rows - (half - children)

            @pl.when(jnp.logical_and(row >= 0, row < half))
            def _():
                act(child, side, lens[side, row], places[side, row])


def read_headers(header, lens, places, steps, most):
    half = lens.shape[1]
    for side in range(2):
        words = header[side].astype(F32)
        used = jnp.int32(1)
        for r in range(half):
            length = jnp.max(words[r : r + 1]).astype(jnp.int32)
            count = jnp.clip(live_tiles(length, steps), 1, most)
            lens[side, r] = count
            places[side, r] = used
            used = used + count


def place_kernel(
    steps, anc_in, sent_a, sent_b, head_a, head_b, held_ref, out_ref, any_ref, more_ref,
    ancs, lens, places, header, own, header_sems, live_sems,
):
    del held_ref
    rows, _, slots, _ = out_ref.shape
    top = pl.ds(0, TILE)
    load_all(
        (anc_in, head_a.at[0, top], head_b.at[0, top], sent_a.at[0, top], sent_b.at[0, top]),
        (ancs, header.at[0], header.at[1], own.at[0], own.at[1]),
        header_sems,
    )
    read_headers(header, lens, places, steps, slots // TILE)

    def each(act):
        def one(child, side, count, place):
            for which, head in enumerate((head_a, head_b)):

                if side != which:
                    continue

                @pl.when(place + count <= HEAD)
                def _():
                    source = head.at[:, tiles(place, count)]
                    target = out_ref.at[child, :, tiles(0, count)]
                    act(pltpu.make_async_copy(source, target, live_sems.at[child]))

        remote_rows(ancs, lens, places, rows, one)

    each(lambda copy: copy.start())
    flag = rows // 2
    both = jnp.maximum(header[...].astype(F32), own[...].astype(F32))
    for side in range(2):
        more_ref[side] = jnp.max(both[side, flag : flag + 1]).astype(jnp.int32)
    any_ref[0] = jnp.maximum(more_ref[0], more_ref[1])
    each(lambda copy: copy.wait())


def place(steps, ancestors, sent, heads, held):
    rows, _, _, hd = held.shape
    half = rows // 2
    return pl.pallas_call(
        functools.partial(place_kernel, steps),
        out_shape=(
            like(held),
            jax.ShapeDtypeStruct((1,), jnp.int32),
            jax.ShapeDtypeStruct((2,), jnp.int32),
        ),
        in_specs=[ANY] * 5 + [HBM],
        out_specs=(HBM, SMEM, SMEM),
        scratch_shapes=[
            pltpu.SMEM((rows,), jnp.int32),
            pltpu.SMEM((2, half), jnp.int32),
            pltpu.SMEM((2, half), jnp.int32),
            pltpu.VMEM((2, TILE, hd), BF16),
            pltpu.VMEM((2, TILE, hd), BF16),
            pltpu.SemaphoreType.DMA((5,)),
            pltpu.SemaphoreType.DMA((rows,)),
        ],
        input_output_aliases={5: 0},
        compiler_params=params(1),
        name="place",
    )(ancestors, *sent, *heads, in_hbm(held))


def place_tails_kernel(
    steps, anc_in, head_a, head_b, tail_a, tail_b, held_ref, out_ref,
    ancs, lens, places, header, header_sems, live_sems,
):
    del held_ref
    rows, _, slots, _ = out_ref.shape
    top = pl.ds(0, TILE)
    load_all(
        (anc_in, head_a.at[0, top], head_b.at[0, top]), (ancs, header.at[0], header.at[1]), header_sems
    )
    read_headers(header, lens, places, steps, slots // TILE)

    def each(act):
        def one(child, side, count, place):
            for which, tail in enumerate((tail_a, tail_b)):

                if side != which:
                    continue

                @pl.when(place + count > HEAD)
                def _():
                    source = tail.at[:, tiles(place - SLACK, count)]
                    target = out_ref.at[child, :, tiles(0, count)]
                    act(pltpu.make_async_copy(source, target, live_sems.at[child]))

        remote_rows(ancs, lens, places, rows, one)

    each(lambda copy: copy.start())
    each(lambda copy: copy.wait())


def place_tails(steps, ancestors, heads, tails, held):
    rows, _, _, hd = held.shape
    half = rows // 2
    return pl.pallas_call(
        functools.partial(place_tails_kernel, steps),
        out_shape=like(held),
        in_specs=[ANY] * 5 + [HBM],
        out_specs=HBM,
        scratch_shapes=[
            pltpu.SMEM((rows,), jnp.int32),
            pltpu.SMEM((2, half), jnp.int32),
            pltpu.SMEM((2, half), jnp.int32),
            pltpu.VMEM((2, TILE, hd), BF16),
            pltpu.SemaphoreType.DMA((3,)),
            pltpu.SemaphoreType.DMA((rows,)),
        ],
        input_output_aliases={5: 0},
        compiler_params=params(1),
        name="place_tails",
    )(ancestors, *heads, *tails, in_hbm(held))


def attend_kernel(
    len_in, cache_ref, nk_in, nv_in, q_ref, pk_ref, pv_ref, w_ref, theirs_ref, ours_ref, app_ref,
    len_ref, nk, nv, small_sems, in_sems, qs, att, wbuf, sems,
):
    rows, steps, _ = q_ref.shape
    heads = q_ref.shape[2] // HD
    slots = app_ref.shape[2]
    chips, tokens, width = theirs_ref.shape
    core = lax.rem(lax.axis_index("tp"), 2)

    def w_copy(k):
        who = jnp.where(k < chips, 1 - core, core)
        cols = pl.ds(pl.multiple_of((2 * lax.rem(k, chips) + who) * width, width), width)
        return pltpu.make_async_copy(w_ref.at[:, cols], wbuf.at[k], sems.at[k])

    @pl.loop(0, rows)
    def _(p):
        pltpu.make_async_copy(cache_ref.at[p], app_ref.at[p], in_sems.at[p]).start()

    @pl.loop(0, 2 * chips)
    def _(k):
        w_copy(k).start()

    load_all((len_in, nk_in, nv_in), (len_ref, nk, nv), small_sems)

    pair = 2 * steps
    groups = rows // 2
    block = heads * pair
    for g in range(groups):
        two = jnp.concatenate([q_ref[2 * g].astype(F32), q_ref[2 * g + 1].astype(F32)], 0)
        for h in range(heads):
            qs[pl.ds((g * heads + h) * pair, pair), :] = two[:, h * HD : (h + 1) * HD]

    for p in range(rows):
        pltpu.make_async_copy(cache_ref.at[p], app_ref.at[p], in_sems.at[p]).wait()
        count = live_tiles(len_ref[p], steps)
        for kv, fresh_ref in ((0, nk), (1, nv)):
            fresh = fresh_ref[p].astype(F32)
            for tile in (jnp.maximum(count - 2, 0), count - 1):
                insert(app_ref, (p, kv, tile_at(tile)), tile, len_ref[p], fresh, steps)

    factor = math.log2(math.e) / math.sqrt(HD)
    per = 4
    big = per * block
    prompt_k = pk_ref[...]
    prompt_v = pv_ref[...]
    r = lax.broadcasted_iota(jnp.int32, (pair, 2 * slots), 0)
    c = lax.broadcasted_iota(jnp.int32, (pair, 2 * slots), 1)
    same = (r // steps) == (c // slots)
    lead = jnp.where(same, lax.rem(c, slots) - lax.rem(r, steps), slots)
    left = c[:1] < slots
    nt = (((1,), (1,)), ((), ()))
    for ch in range(groups // per):
        q = qs[pl.ds(ch * big, big), :].astype(BF16)
        s_prompt = lax.dot_general(q, prompt_k, nt, preferred_element_type=F32)
        s_own = []
        for i in range(per):
            g = ch * per + i
            keys = app_ref[2 * g : 2 * g + 2, 0].reshape(2 * slots, HD)
            s = lax.dot_general(
                q[i * block : (i + 1) * block], keys, nt, preferred_element_type=F32
            )
            limit = jnp.where(left, len_ref[2 * g], len_ref[2 * g + 1])
            seen = lead <= limit
            s = s.reshape(heads, pair, 2 * slots)
            s_own.append(jnp.where(seen[None], s, -1e30).reshape(block, 2 * slots))
        s_own = jnp.concatenate(s_own, 0)
        top = jnp.maximum(
            jnp.max(s_prompt, axis=1, keepdims=True), jnp.max(s_own, axis=1, keepdims=True)
        )
        e_prompt = jnp.exp2((s_prompt - top) * factor)
        e_own = jnp.exp2((s_own - top) * factor)
        total = jnp.sum(e_prompt, axis=1, keepdims=True) + jnp.sum(e_own, axis=1, keepdims=True)
        o = jnp.dot(e_prompt.astype(BF16), prompt_v, preferred_element_type=F32)
        e_own = e_own.astype(BF16)
        own = []
        for i in range(per):
            g = ch * per + i
            values = app_ref[2 * g : 2 * g + 2, 1].reshape(2 * slots, HD)
            own.append(
                jnp.dot(
                    e_own[i * block : (i + 1) * block], values, preferred_element_type=F32
                )
            )
        o = (o + jnp.concatenate(own, 0)) / total
        for i in range(per):
            g = ch * per + i
            for h in range(heads):
                at = i * block + h * pair
                att[pl.ds(g * pair, pair), h * HD : (h + 1) * HD] = o[at : at + pair]

    attended = att[...].astype(BF16)
    for k in range(2 * chips):
        w_copy(jnp.int32(k)).wait()
        part = jnp.dot(attended, wbuf[k], preferred_element_type=F32)
        if k < chips:
            theirs_ref[k] = part.astype(BF16)
        else:
            ours_ref[k - chips] = part


def attend(
    lengths, cache, new_keys, new_values, queries, prompt_keys, prompt_values, out_weight, chips, width
):
    rows, steps, q_cols = queries.shape
    tokens = rows * steps
    flops = 2 * 2 * tokens * q_cols * prompt_keys.shape[0] + 2 * tokens * out_weight.size
    return pl.pallas_call(
        attend_kernel,
        out_shape=(
            jax.ShapeDtypeStruct((chips, tokens, width), BF16),
            jax.ShapeDtypeStruct((chips, tokens, width), F32),
            like(cache),
        ),
        in_specs=[ANY, HBM, ANY, ANY, VMEM, VMEM, VMEM, HBM],
        out_specs=(VMEM, VMEM, VMEM),
        scratch_shapes=[
            pltpu.SMEM((rows,), jnp.int32),
            pltpu.VMEM(new_keys.shape, BF16),
            pltpu.VMEM(new_values.shape, BF16),
            pltpu.SemaphoreType.DMA((3,)),
            pltpu.SemaphoreType.DMA((rows,)),
            pltpu.VMEM((tokens * q_cols // HD, HD), F32),
            pltpu.VMEM((tokens, q_cols), F32),
            pltpu.VMEM((2 * chips, out_weight.shape[0], width), BF16),
            pltpu.SemaphoreType.DMA((2 * chips,)),
        ],
        compiler_params=params(40),
        cost_estimate=pl.CostEstimate(
            flops=flops, bytes_accessed=2 * out_weight.size, transcendentals=0
        ),
        name="attend",
    )(
        lengths, in_hbm(cache), new_keys, new_values, queries, prompt_keys, prompt_values,
        in_hbm(out_weight),
    )


def pair_sum_kernel(ours_ref, got_ref, keep_ref, *send_refs):
    chips = ours_ref.shape[0]
    me = lax.axis_index("tp") // 2
    for k in range(chips):
        at = lax.rem(me + k, chips)
        both = ours_ref[at] + got_ref[at].astype(F32)
        if k == 0:
            keep_ref[...] = both
        else:
            send_refs[k - 1][...] = both.astype(BF16)


def pair_sum(ours, got):
    chips, tokens, width = ours.shape
    return pl.pallas_call(
        pair_sum_kernel,
        out_shape=(jax.ShapeDtypeStruct((tokens, width), F32),)
        + (jax.ShapeDtypeStruct((tokens, width), BF16),) * (chips - 1),
        in_specs=[VMEM, VMEM],
        out_specs=(VMEM,) * chips,
        compiler_params=params(2),
        name="pair_sum",
    )(ours, got)


def chip_sum_kernel(keep_ref, *refs):
    got_refs, out_ref = refs[:-1], refs[-1]
    rows, steps, _ = out_ref.shape
    total = keep_ref[...]
    for ref in got_refs:
        total = total + ref[...].astype(F32)
    total = total.astype(BF16)
    for p in range(rows):
        out_ref[p] = total[p * steps : (p + 1) * steps]


def chip_sum(keep, got, rows):
    tokens, width = keep.shape
    return pl.pallas_call(
        chip_sum_kernel,
        out_shape=jax.ShapeDtypeStruct((rows, tokens // rows, width), BF16),
        in_specs=[VMEM] * (1 + len(got)),
        out_specs=VMEM,
        compiler_params=params(2),
        name="chip_sum",
    )(keep, *got)


def body(
    queries,
    new_keys,
    new_values,
    prompt_keys,
    prompt_values,
    suffix_cache,
    lengths,
    ancestors,
    out_weight,
):
    rows, steps, _ = queries.shape
    doms = lax.axis_size("dom")
    tps = lax.axis_size("tp")
    chips = tps // 2
    width = out_weight.shape[1] // tps

    packed = first(lengths, suffix_cache, new_keys, new_values)
    even_pairs = [(i, i ^ 1) for i in range(doms)]
    odd_pairs = [(i, i + 1) for i in range(1, doms - 1, 2)]
    routes = (even_pairs, odd_pairs + [(j, i) for i, j in odd_pairs])
    heads = [lax.ppermute(head, "dom", route) for head, route in zip(packed[:2], routes)]

    theirs, ours, app = attend(
        lengths, suffix_cache, new_keys, new_values, queries, prompt_keys, prompt_values, out_weight,
        chips, width,
    )
    got = lax.ppermute(theirs, "tp", [(i, i ^ 1) for i in range(tps)])
    mine, *send = pair_sum(ours, got)
    arrived = [
        lax.ppermute(send[k - 1], "tp", [(i, (i + 2 * k) % tps) for i in range(tps)])
        for k in (2, 3, 1)
    ]
    mixed = chip_sum(mine, arrived, rows)
    held = keep(steps, lengths, ancestors, app)

    held, some, more = place(steps, ancestors, packed[:2], heads, held)

    def exchange(held, *tails):
        got = [
            lax.cond(
                flag > 0, lambda v, route=route: lax.ppermute(v, "dom", route), lambda v: v, tail
            )
            for flag, tail, route in zip((more[0], more[1]), tails, routes)
        ]
        return place_tails(steps, ancestors, heads, got, held)

    new_cache = lax.cond(some[0] > 0, exchange, lambda held, *tails: held, held, *packed[2:])
    return (mixed, new_cache)


def solution(mesh):
    in_specs = (
        P("dom", None, "tp"),
        P("dom", None, "tp"),
        P("dom", None, "tp"),
        P(None, "tp"),
        P(None, "tp"),
        P("dom", None, None, "tp"),
        P("dom"),
        P("dom"),
        P("tp", None),
    )
    out_specs = (P("dom", None, "tp"), P("dom", None, None, "tp"))
    return jax.shard_map(body, mesh=mesh, in_specs=in_specs, out_specs=out_specs, check_vma=False)
```

time: 44.6 us -> 35.2 us (0.79)
  local copies, waits for them, and re-layouts: 7.96 us -> 0.03 us
  waiting for transfers between devices: 5.84 us -> 4.44 us
  between operations: 0.78 us -> 1.41 us
  starting transfers between devices: 15.2 us -> 14.6 us
    unnamed x22 -> x14, local copies, waits for them, and re-layouts: 7.73 us -> 0.03 us
    ppermute x5, waiting for transfers between devices: 4.32 us -> 2.92 us  [the longest x3 2.32 us: body(): lax.ppermute(send[k - 1], 'tp', [(i, (i + 2 * k) % tps) for i in range(tp...]
    ppermute x5, starting transfers between devices: 15.1 us -> 14.5 us  [the longest x2 9.22 us: body(): lax.ppermute(head, 'dom', route)]
    pallas_call x2 -> x3, Pallas kernels: 7.04 us -> 7.19 us  [the longest x1 2.58 us: first(): pl.pallas_call(first_kernel, out_shape=(head, head, tail, tail), in_specs...]
  transfers between devices with their start and end apart: 6 -> 6, of which waited for: 4 -> 4; matrix products, arithmetic and copies ran while one was open for 0% -> 0% of each run, Pallas kernels for 17% -> 27%
where the time goes in v2:
time: 35.2 us; the launch traced here: 35.1 us
  Pallas kernels  14.6 us (41%)
  starting transfers between devices  14.6 us (41%)
  waiting for transfers between devices  4.44 us (13%)
  between operations  1.41 us (4%)
    ppermute x2, starting transfers between devices, body(): lax.ppermute(head, 'dom', route)  9.22 us
    pallas_call x1, Pallas kernels, attend(): pl.pallas_call(attend_kernel, out_shape=(jax.ShapeDtypeStruct((chips, tok...  6.7 us
    ppermute x3, starting transfers between devices, body(): lax.ppermute(send[k - 1], 'tp', [(i, (i + 2 * k) % tps) for i in range(tp...  5.3 us
    pallas_call x1, Pallas kernels, first(): pl.pallas_call(first_kernel, out_shape=(head, head, tail, tail), in_specs...  2.58 us
    pallas_call x1, Pallas kernels, place(): pl.pallas_call(functools.partial(place_kernel, steps), out_shape=(like(he...  2.44 us
    ppermute x3, waiting for transfers between devices, body(): lax.ppermute(send[k - 1], 'tp', [(i, (i + 2 * k) % tps) for i in range(tp...  2.32 us
    pallas_call x1, Pallas kernels, keep(): pl.pallas_call(functools.partial(keep_kernel, steps), out_shape=like(app)...  2.17 us
    ppermute x1, waiting for transfers between devices, body(): got = lax.ppermute(theirs, 'tp', [(i, i ^ 1) for i in range(tps)])  1.52 us
  transfers between devices with their start and end apart: 6, of which 4 were waited for; matrix products, arithmetic and copies ran while one was open for 0% of the time, Pallas kernels for 27%

profile of v2, /device:TPU:6, one launch (start us, length us, event | category | flops | bytes accessed | tf_op | source)
XLA Modules:
  0.0 35.1 jit_solution(4415337979139779065)
XLA Ops:
  0.6 0.0 copy-start.5
  0.6 0.0 copy-start.4
  0.7 0.0 copy-start.3
  0.7 0.0 copy-start.1
  0.7 0.0 copy-start
  0.7 0.0 copy-start.2
  0.7 2.6 %first.1 = (bf16[2,1744,128]{2,1,0:T(8,128)(2,1)S(1)}, bf16[2,1744,128]{2,1,0:T(8,128)(2,1)S(1)}, bf16[2,560,128]{2,1,0:T(8,128)(2,1)S(1)}, bf16[2,560,128]{2,1,0:T(8,128)(2,1)S(1)}) custom-call(s32[16]{0:T(128)} %len_in.3, bf16[16,2,256,128]{3,2,1,0:T(8,128)(2,1)} %cache_ref.3, bf16[16,4,128]{2,1,0:T(4,128)(2,1)} %nk_hbm.1, bf16[16,4,128]{2,1,0:T(4,128)(2,1)} %nv_hbm.1), custom_call_target="tpu_custom_call" | custom-call | tf_op jit(solution)/shard_map/first/pallas_call | solution.py:169
  3.3 2.0 %collective-permute-start.6 = (bf16[2,1744,128]{2,1,0:T(8,128)(2,1)S(1)}, bf16[2,1744,128]{2,1,0:T(8,128)(2,1)S(1)}, u32[]{:S(2)}, u32[]{:S(2)}) collective-permute-start(bf16[2,1744,128]{2,1,0:T(8,128)(2,1)S(1)} %get-tuple-element.57.sent_a), channel_id=1, source_target_pairs={{0,8},{8,0},{16,24},{24,16},{32,40},{40,32},{48,56},{56,48},{64,72... | collective-permute-start | bytes 2678792 | tf_op jit(solution)/shard_map/ppermute | solution.py:596
  5.3 7.2 %collective-permute-start.7 = (bf16[2,1744,128]{2,1,0:T(8,128)(2,1)S(1)}, bf16[2,1744,128]{2,1,0:T(8,128)(2,1)S(1)}, u32[]{:S(2)}, u32[]{:S(2)}) collective-permute-start(bf16[2,1744,128]{2,1,0:T(8,128)(2,1)S(1)} %get-tuple-element.58.sent_b), channel_id=1, source_target_pairs={{8,16},{24,32},{40,48},{56,64},{72,80},{88,96},{104,112},{120,128}... | collective-permute-start | bytes 2678792 | tf_op jit(solution)/shard_map/ppermute | solution.py:596
  12.5 0.0 copy-done.5
  12.6 6.7 %attend.1 = (bf16[4,64,512]{2,1,0:T(8,128)(2,1)S(1)}, f32[4,64,512]{2,1,0:T(8,128)S(1)}, bf16[16,2,256,128]{3,2,1,0:T(8,128)(2,1)S(1)}) custom-call(s32[16]{0:T(128)S(1)} %copy-done.5, bf16[16,2,256,128]{3,2,1,0:T(8,128)(2,1)} %cache_ref.3, bf16[16,4,128]{2,1,0:T(4,128)(2,1)S(1)} %copy-done.3, bf16[16,4,128]{2,1,0:T(4,128)(2,1)S(1)} %copy-done.4, ...), custom_call_target="tpu_custom_call" | custom-call | flops 1073741824 | bytes 8388608 | tf_op jit(solution)/shard_map/attend/pallas_call | solution.py:496
  19.3 0.1 collective-permute-start.2
  19.4 1.5 %collective-permute-done.2.got_ref = bf16[4,64,512]{2,1,0:T(8,128)(2,1)S(1)} collective-permute-done((bf16[4,64,512]{2,1,0:T(8,128)(2,1)S(1)}, bf16[4,64,512]{2,1,0:T(8,128)(2,1)S(1)}, u32[]{:S(2)}, u32[]{:S(2)}) %collective-permute-start.2) | collective-permute-done | bytes 262176 | tf_op jit(solution)/shard_map/ppermute | solution.py:602
  21.0 3.3 %collective-permute-start.3 = (bf16[64,512]{1,0:T(8,128)(2,1)S(1)}, bf16[64,512]{1,0:T(8,128)(2,1)S(1)}, u32[]{:S(2)}, u32[]{:S(2)}) collective-permute-start(bf16[64,512]{1,0:T(8,128)(2,1)S(1)} %get-tuple-element.54), channel_id=1, source_target_pairs={{0,4},{1,5},{2,6},{3,7},{4,0},{5,1},{6,2},{7,3},{8,12},{9,13},{10,... | collective-permute-start | bytes 196616 | tf_op jit(solution)/shard_map/ppermute | solution.py:605
  24.2 1.1 %collective-permute-start.4 = (bf16[64,512]{1,0:T(8,128)(2,1)S(1)}, bf16[64,512]{1,0:T(8,128)(2,1)S(1)}, u32[]{:S(2)}, u32[]{:S(2)}) collective-permute-start(bf16[64,512]{1,0:T(8,128)(2,1)S(1)} %get-tuple-element.55), channel_id=1, source_target_pairs={{0,6},{1,7},{2,0},{3,1},{4,2},{5,3},{6,4},{7,5},{8,14},{9,15},{10,... | collective-permute-start | bytes 196616 | tf_op jit(solution)/shard_map/ppermute | solution.py:605
  25.3 1.0 %collective-permute-start.5 = (bf16[64,512]{1,0:T(8,128)(2,1)S(1)}, bf16[64,512]{1,0:T(8,128)(2,1)S(1)}, u32[]{:S(2)}, u32[]{:S(2)}) collective-permute-start(bf16[64,512]{1,0:T(8,128)(2,1)S(1)} %get-tuple-element.56), channel_id=1, source_target_pairs={{0,2},{1,3},{2,4},{3,5},{4,6},{5,7},{6,0},{7,1},{8,10},{9,11},{10,... | collective-permute-start | bytes 196616 | tf_op jit(solution)/shard_map/ppermute | solution.py:605
  26.3 2.2 %keep.1.held_ref = bf16[16,2,256,128]{3,2,1,0:T(8,128)(2,1)} custom-call(s32[16]{0:T(128)S(1)} %copy-done.5, s32[16]{0:T(128)S(1)} %copy-done.6, bf16[16,2,256,128]{3,2,1,0:T(8,128)(2,1)S(1)} %get-tuple-element.59.app_ref), custom_call_target="tpu_custom_call" | custom-call | tf_op jit(solution)/shard_map/keep/pallas_call | solution.py:225
  28.4 0.0 collective-permute-done.3.refs_0_
  28.5 0.1 collective-permute-done.4.refs_1_
  28.6 2.2 %collective-permute-done.5.refs_2_ = bf16[64,512]{1,0:T(8,128)(2,1)S(1)} collective-permute-done((bf16[64,512]{1,0:T(8,128)(2,1)S(1)}, bf16[64,512]{1,0:T(8,128)(2,1)S(1)}, u32[]{:S(2)}, u32[]{:S(2)}) %collective-permute-start.5) | collective-permute-done | bytes 65568 | tf_op jit(solution)/shard_map/ppermute | solution.py:605
  30.8 0.7 %chip_sum.1 = bf16[16,4,512]{2,1,0:T(4,128)(2,1)} custom-call(f32[64,512]{1,0:T(8,128)S(1)} %get-tuple-element.53.keep_ref, bf16[64,512]{1,0:T(8,128)(2,1)S(1)} %collective-permute-done.3.refs_0_, bf16[64,512]{1,0:T(8,128)(2,1)S(1)} %collective-permute-done.4.refs_1_, bf16[64,512]{1,0:T(8,128)(2,1)S(1)} %collective-permute-done.5.refs_2_), custom_call_target="tpu_custom_call" | custom-call | tf_op jit(solution)/shard_map/chip_sum/pallas_call | solution.py:565
  31.4 0.0 collective-permute-done.6.head_a
  31.4 0.6 %collective-permute-done.7.head_b = bf16[2,1744,128]{2,1,0:T(8,128)(2,1)S(1)} collective-permute-done((bf16[2,1744,128]{2,1,0:T(8,128)(2,1)S(1)}, bf16[2,1744,128]{2,1,0:T(8,128)(2,1)S(1)}, u32[]{:S(2)}, u32[]{:S(2)}) %collective-permute-start.7) | collective-permute-done | bytes 892960 | tf_op jit(solution)/shard_map/ppermute | solution.py:596
  32.0 2.4 %place.1 = (bf16[16,2,256,128]{3,2,1,0:T(8,128)(2,1)}, s32[1]{0:T(128)}, s32[2]{0:T(128)S(1)}) custom-call(s32[16]{0:T(128)S(1)} %copy-done.6, bf16[2,1744,128]{2,1,0:T(8,128)(2,1)S(1)} %get-tuple-element.57.sent_a, bf16[2,1744,128]{2,1,0:T(8,128)(2,1)S(1)} %get-tuple-element.58.sent_b, ...), custom_call_target="tpu_custom_call", output_to_operand_aliasing={{0}: (5, {})} | custom-call | tf_op jit(solution)/shard_map/place/pallas_call | solution.py:312
  (9 shorter events, 0.1 us)
Async XLA Ops:
  0.6 11.9 %copy-start.5 = (s32[16]{0:T(128)S(1)}, s32[16]{0:T(128)}, u32[]{:S(2)}) copy-start(s32[16]{0:T(128)} %len_in.3) | copy-start | bytes 196
  0.6 11.9 %copy-start.4 = (bf16[16,4,128]{2,1,0:T(4,128)(2,1)S(1)}, bf16[16,4,128]{2,1,0:T(4,128)(2,1)}, u32[]{:S(2)}) copy-start(bf16[16,4,128]{2,1,0:T(4,128)(2,1)} %nv_hbm.1) | copy-start | bytes 49156
  0.7 11.9 %copy-start.3 = (bf16[16,4,128]{2,1,0:T(4,128)(2,1)S(1)}, bf16[16,4,128]{2,1,0:T(4,128)(2,1)}, u32[]{:S(2)}) copy-start(bf16[16,4,128]{2,1,0:T(4,128)(2,1)} %nk_hbm.1) | copy-start | bytes 49156
  0.7 11.9 %copy-start.1 = (bf16[2048,128]{1,0:T(8,128)(2,1)S(1)}, bf16[2048,128]{1,0:T(8,128)(2,1)}, u32[]{:S(2)}) copy-start(bf16[2048,128]{1,0:T(8,128)(2,1)} %pv_ref.1) | copy-start | bytes 1572868
  0.7 11.9 %copy-start = (bf16[2048,128]{1,0:T(8,128)(2,1)S(1)}, bf16[2048,128]{1,0:T(8,128)(2,1)}, u32[]{:S(2)}) copy-start(bf16[2048,128]{1,0:T(8,128)(2,1)} %pk_ref.1) | copy-start | bytes 1572868
  0.7 11.9 %copy-start.2 = (bf16[16,4,1024]{2,1,0:T(4,128)(2,1)S(1)}, bf16[16,4,1024]{2,1,0:T(4,128)(2,1)}, u32[]{:S(2)}) copy-start(bf16[16,4,1024]{2,1,0:T(4,128)(2,1)} %q_ref.1) | copy-start | bytes 393220
  3.3 28.2 %collective-permute-start.6 = (bf16[2,1744,128]{2,1,0:T(8,128)(2,1)S(1)}, bf16[2,1744,128]{2,1,0:T(8,128)(2,1)S(1)}, u32[]{:S(2)}, u32[]{:S(2)}) collective-permute-start(bf16[2,1744,128]{2,1,0:T(8,128)(2,1)S(1)} %get-tuple-element.57.sent_a), channel_id=1, source_target_pairs={{0,8},{8,0},{16,24},{24,16},{32,40},{40,32},{48,56},{56,48},{64,72... | collective-permute-start | bytes 2678792 | tf_op jit(solution)/shard_map/ppermute | solution.py:596
  5.3 20.9 %copy-start.6 = (s32[16]{0:T(128)S(1)}, s32[16]{0:T(128)}, u32[]{:S(2)}) copy-start(s32[16]{0:T(128)} %anc_in.3) | copy-start | bytes 196
  5.3 26.7 %collective-permute-start.7 = (bf16[2,1744,128]{2,1,0:T(8,128)(2,1)S(1)}, bf16[2,1744,128]{2,1,0:T(8,128)(2,1)S(1)}, u32[]{:S(2)}, u32[]{:S(2)}) collective-permute-start(bf16[2,1744,128]{2,1,0:T(8,128)(2,1)S(1)} %get-tuple-element.58.sent_b), channel_id=1, source_target_pairs={{8,16},{24,32},{40,48},{56,64},{72,80},{88,96},{104,112},{120,128}... | collective-permute-start | bytes 2678792 | tf_op jit(solution)/shard_map/ppermute | solution.py:596
  19.3 1.6 %collective-permute-start.2 = (bf16[4,64,512]{2,1,0:T(8,128)(2,1)S(1)}, bf16[4,64,512]{2,1,0:T(8,128)(2,1)S(1)}, u32[]{:S(2)}, u32[]{:S(2)}) collective-permute-start(bf16[4,64,512]{2,1,0:T(8,128)(2,1)S(1)} %get-tuple-element.52), channel_id=1, source_target_pairs={{0,1},{1,0},{2,3},{3,2},{4,5},{5,4},{6,7},{7,6},{8,9},{9,8},{10,11... | collective-permute-start | bytes 786440 | tf_op jit(solution)/shard_map/ppermute | solution.py:602
  21.0 7.5 %collective-permute-start.3 = (bf16[64,512]{1,0:T(8,128)(2,1)S(1)}, bf16[64,512]{1,0:T(8,128)(2,1)S(1)}, u32[]{:S(2)}, u32[]{:S(2)}) collective-permute-start(bf16[64,512]{1,0:T(8,128)(2,1)S(1)} %get-tuple-element.54), channel_id=1, source_target_pairs={{0,4},{1,5},{2,6},{3,7},{4,0},{5,1},{6,2},{7,3},{8,12},{9,13},{10,... | collective-permute-start | bytes 196616 | tf_op jit(solution)/shard_map/ppermute | solution.py:605
  24.2 4.3 %collective-permute-start.4 = (bf16[64,512]{1,0:T(8,128)(2,1)S(1)}, bf16[64,512]{1,0:T(8,128)(2,1)S(1)}, u32[]{:S(2)}, u32[]{:S(2)}) collective-permute-start(bf16[64,512]{1,0:T(8,128)(2,1)S(1)} %get-tuple-element.55), channel_id=1, source_target_pairs={{0,6},{1,7},{2,0},{3,1},{4,2},{5,3},{6,4},{7,5},{8,14},{9,15},{10,... | collective-permute-start | bytes 196616 | tf_op jit(solution)/shard_map/ppermute | solution.py:605
  25.3 5.5 %collective-permute-start.5 = (bf16[64,512]{1,0:T(8,128)(2,1)S(1)}, bf16[64,512]{1,0:T(8,128)(2,1)S(1)}, u32[]{:S(2)}, u32[]{:S(2)}) collective-permute-start(bf16[64,512]{1,0:T(8,128)(2,1)S(1)} %get-tuple-element.56), channel_id=1, source_target_pairs={{0,2},{1,3},{2,4},{3,5},{4,6},{5,7},{6,0},{7,1},{8,10},{9,11},{10,... | collective-permute-start | bytes 196616 | tf_op jit(solution)/shard_map/ppermute | solution.py:605

commit v3 on v2

--- a/solution.py
+++ b/solution.py
@@ -590,10 +590,13 @@
     width = out_weight.shape[1] // tps
 
     packed = first(lengths, suffix_cache, new_keys, new_values)
-    even_pairs = [(i, i ^ 1) for i in range(doms)]
-    odd_pairs = [(i, i + 1) for i in range(1, doms - 1, 2)]
-    routes = (even_pairs, odd_pairs + [(j, i) for i, j in odd_pairs])
-    heads = [lax.ppermute(head, "dom", route) for head, route in zip(packed[:2], routes)]
+    def partner(i, side):
+        dom, tp = divmod(i, tps)
+        other = dom ^ 1 if side == 0 else (dom + 1) // 2 * 4 - 1 - dom
+        return other * tps + tp if 0 <= other < doms else i ^ 1
+
+    routes = [[(i, partner(i, side)) for i in range(doms * tps)] for side in range(2)]
+    heads = [lax.ppermute(head, ("dom", "tp"), route) for head, route in zip(packed[:2], routes)]
 
     theirs, ours, app = attend(
         lengths, suffix_cache, new_keys, new_values, queries, prompt_keys, prompt_values, out_weight,
@@ -613,7 +616,7 @@
     def exchange(held, *tails):
         got = [
             lax.cond(
-                flag > 0, lambda v, route=route: lax.ppermute(v, "dom", route), lambda v: v, tail
+                flag > 0, lambda v, route=route: lax.ppermute(v, ("dom", "tp"), route), lambda v: v, tail
             )
             for flag, tail, route in zip((more[0], more[1]), tails, routes)
         ]

time: 35.2 us -> 33.2 us (0.943)
  starting transfers between devices: 14.6 us -> 12.6 us
    ppermute x2, starting transfers between devices: 9.22 us -> 7.24 us  [body(): lax.ppermute(head, ('dom', 'tp'), route)]
  transfers between devices with their start and end apart: 6 -> 6, of which waited for: 4 -> 4; matrix products, arithmetic and copies ran while one was open for 0% -> 0% of each run, Pallas kernels for 27% -> 29%
where the time goes in v3:
time: 33.2 us; the launch traced here: 33 us
  Pallas kernels  14.5 us (44%)
  starting transfers between devices  12.6 us (38%)
  waiting for transfers between devices  4.48 us (13%)
  between operations  1.38 us (4%)
    ppermute x2, starting transfers between devices, body(): lax.ppermute(head, ('dom', 'tp'), route)  7.24 us
    pallas_call x1, Pallas kernels, attend(): pl.pallas_call(attend_kernel, out_shape=(jax.ShapeDtypeStruct((chips, tok...  6.71 us
    ppermute x3, starting transfers between devices, body(): lax.ppermute(send[k - 1], 'tp', [(i, (i + 2 * k) % tps) for i in range(tp...  5.31 us
    pallas_call x1, Pallas kernels, first(): pl.pallas_call(first_kernel, out_shape=(head, head, tail, tail), in_specs...  2.56 us
    pallas_call x1, Pallas kernels, place(): pl.pallas_call(functools.partial(place_kernel, steps), out_shape=(like(he...  2.37 us
    ppermute x3, waiting for transfers between devices, body(): lax.ppermute(send[k - 1], 'tp', [(i, (i + 2 * k) % tps) for i in range(tp...  2.32 us
    pallas_call x1, Pallas kernels, keep(): pl.pallas_call(functools.partial(keep_kernel, steps), out_shape=like(app)...  2.17 us
    ppermute x1, waiting for transfers between devices, body(): got = lax.ppermute(theirs, 'tp', [(i, i ^ 1) for i in range(tps)])  1.52 us
  transfers between devices with their start and end apart: 6, of which 4 were waited for; matrix products, arithmetic and copies ran while one was open for 0% of the time, Pallas kernels for 29%

profile of v3, /device:TPU:6, one launch (start us, length us, event | category | flops | bytes accessed | tf_op | source)
XLA Modules:
  0.0 33.0 jit_solution(3123406484447629098)
XLA Ops:
  0.6 0.0 copy-start.5
  0.6 0.0 copy-start.4
  0.7 0.0 copy-start.3
  0.7 0.0 copy-start.1
  0.7 2.6 %first.1 = (bf16[2,1744,128]{2,1,0:T(8,128)(2,1)S(1)}, bf16[2,1744,128]{2,1,0:T(8,128)(2,1)S(1)}, bf16[2,560,128]{2,1,0:T(8,128)(2,1)S(1)}, bf16[2,560,128]{2,1,0:T(8,128)(2,1)S(1)}) custom-call(s32[16]{0:T(128)} %len_in.3, bf16[16,2,256,128]{3,2,1,0:T(8,128)(2,1)} %cache_ref.3, bf16[16,4,128]{2,1,0:T(4,128)(2,1)} %nk_hbm.1, bf16[16,4,128]{2,1,0:T(4,128)(2,1)} %nv_hbm.1), custom_call_target="tpu_custom_call" | custom-call | tf_op jit(solution)/shard_map/first/pallas_call | solution.py:169
  3.3 2.1 %collective-permute-start.6 = (bf16[2,1744,128]{2,1,0:T(8,128)(2,1)S(1)}, bf16[2,1744,128]{2,1,0:T(8,128)(2,1)S(1)}, u32[]{:S(2)}, u32[]{:S(2)}) collective-permute-start(bf16[2,1744,128]{2,1,0:T(8,128)(2,1)S(1)} %get-tuple-element.57.sent_a), channel_id=1, source_target_pairs={{0,8},{1,9},{2,10},{3,11},{4,12},{5,13},{6,14},{7,15},{8,0},{9,1},... | collective-permute-start | bytes 2678792 | tf_op jit(solution)/shard_map/ppermute | solution.py:599
  5.3 5.2 %collective-permute-start.7 = (bf16[2,1744,128]{2,1,0:T(8,128)(2,1)S(1)}, bf16[2,1744,128]{2,1,0:T(8,128)(2,1)S(1)}, u32[]{:S(2)}, u32[]{:S(2)}) collective-permute-start(bf16[2,1744,128]{2,1,0:T(8,128)(2,1)S(1)} %get-tuple-element.58.sent_b), channel_id=1, source_target_pairs={{0,1},{1,0},{2,3},{3,2},{4,5},{5,4},{6,7},{7,6},{8,16},{9,17},{10,... | collective-permute-start | bytes 2678792 | tf_op jit(solution)/shard_map/ppermute | solution.py:599
  10.5 0.0 copy-done.5
  10.5 0.0 copy-done
  10.5 0.0 copy-done.2
  10.5 6.7 %attend.1 = (bf16[4,64,512]{2,1,0:T(8,128)(2,1)S(1)}, f32[4,64,512]{2,1,0:T(8,128)S(1)}, bf16[16,2,256,128]{3,2,1,0:T(8,128)(2,1)S(1)}) custom-call(s32[16]{0:T(128)S(1)} %copy-done.5, bf16[16,2,256,128]{3,2,1,0:T(8,128)(2,1)} %cache_ref.3, bf16[16,4,128]{2,1,0:T(4,128)(2,1)S(1)} %copy-done.3, bf16[16,4,128]{2,1,0:T(4,128)(2,1)S(1)} %copy-done.4, ...), custom_call_target="tpu_custom_call" | custom-call | flops 1073741824 | bytes 8388608 | tf_op jit(solution)/shard_map/attend/pallas_call | solution.py:496
  17.2 0.1 collective-permute-start.2
  17.3 1.5 %collective-permute-done.2.got_ref = bf16[4,64,512]{2,1,0:T(8,128)(2,1)S(1)} collective-permute-done((bf16[4,64,512]{2,1,0:T(8,128)(2,1)S(1)}, bf16[4,64,512]{2,1,0:T(8,128)(2,1)S(1)}, u32[]{:S(2)}, u32[]{:S(2)}) %collective-permute-start.2) | collective-permute-done | bytes 262176 | tf_op jit(solution)/shard_map/ppermute | solution.py:605
  18.9 3.3 %collective-permute-start.3 = (bf16[64,512]{1,0:T(8,128)(2,1)S(1)}, bf16[64,512]{1,0:T(8,128)(2,1)S(1)}, u32[]{:S(2)}, u32[]{:S(2)}) collective-permute-start(bf16[64,512]{1,0:T(8,128)(2,1)S(1)} %get-tuple-element.54), channel_id=1, source_target_pairs={{0,4},{1,5},{2,6},{3,7},{4,0},{5,1},{6,2},{7,3},{8,12},{9,13},{10,... | collective-permute-start | bytes 196616 | tf_op jit(solution)/shard_map/ppermute | solution.py:608
  22.2 1.1 %collective-permute-start.4 = (bf16[64,512]{1,0:T(8,128)(2,1)S(1)}, bf16[64,512]{1,0:T(8,128)(2,1)S(1)}, u32[]{:S(2)}, u32[]{:S(2)}) collective-permute-start(bf16[64,512]{1,0:T(8,128)(2,1)S(1)} %get-tuple-element.55), channel_id=1, source_target_pairs={{0,6},{1,7},{2,0},{3,1},{4,2},{5,3},{6,4},{7,5},{8,14},{9,15},{10,... | collective-permute-start | bytes 196616 | tf_op jit(solution)/shard_map/ppermute | solution.py:608
  23.2 1.0 %collective-permute-start.5 = (bf16[64,512]{1,0:T(8,128)(2,1)S(1)}, bf16[64,512]{1,0:T(8,128)(2,1)S(1)}, u32[]{:S(2)}, u32[]{:S(2)}) collective-permute-start(bf16[64,512]{1,0:T(8,128)(2,1)S(1)} %get-tuple-element.56), channel_id=1, source_target_pairs={{0,2},{1,3},{2,4},{3,5},{4,6},{5,7},{6,0},{7,1},{8,10},{9,11},{10,... | collective-permute-start | bytes 196616 | tf_op jit(solution)/shard_map/ppermute | solution.py:608
  24.2 2.2 %keep.1.held_ref = bf16[16,2,256,128]{3,2,1,0:T(8,128)(2,1)} custom-call(s32[16]{0:T(128)S(1)} %copy-done.5, s32[16]{0:T(128)S(1)} %copy-done.6, bf16[16,2,256,128]{3,2,1,0:T(8,128)(2,1)S(1)} %get-tuple-element.59.app_ref), custom_call_target="tpu_custom_call" | custom-call | tf_op jit(solution)/shard_map/keep/pallas_call | solution.py:225
  26.4 0.0 collective-permute-done.3.refs_0_
  26.4 0.1 collective-permute-done.4.refs_1_
  26.5 2.2 %collective-permute-done.5.refs_2_ = bf16[64,512]{1,0:T(8,128)(2,1)S(1)} collective-permute-done((bf16[64,512]{1,0:T(8,128)(2,1)S(1)}, bf16[64,512]{1,0:T(8,128)(2,1)S(1)}, u32[]{:S(2)}, u32[]{:S(2)}) %collective-permute-start.5) | collective-permute-done | bytes 65568 | tf_op jit(solution)/shard_map/ppermute | solution.py:608
  28.7 0.7 %chip_sum.1 = bf16[16,4,512]{2,1,0:T(4,128)(2,1)} custom-call(f32[64,512]{1,0:T(8,128)S(1)} %get-tuple-element.53.keep_ref, bf16[64,512]{1,0:T(8,128)(2,1)S(1)} %collective-permute-done.3.refs_0_, bf16[64,512]{1,0:T(8,128)(2,1)S(1)} %collective-permute-done.4.refs_1_, bf16[64,512]{1,0:T(8,128)(2,1)S(1)} %collective-permute-done.5.refs_2_), custom_call_target="tpu_custom_call" | custom-call | tf_op jit(solution)/shard_map/chip_sum/pallas_call | solution.py:565
  29.4 0.0 collective-permute-done.6.head_a
  29.4 0.6 %collective-permute-done.7.head_b = bf16[2,1744,128]{2,1,0:T(8,128)(2,1)S(1)} collective-permute-done((bf16[2,1744,128]{2,1,0:T(8,128)(2,1)S(1)}, bf16[2,1744,128]{2,1,0:T(8,128)(2,1)S(1)}, u32[]{:S(2)}, u32[]{:S(2)}) %collective-permute-start.7) | collective-permute-done | bytes 892960 | tf_op jit(solution)/shard_map/ppermute | solution.py:599
  30.0 2.4 %place.1 = (bf16[16,2,256,128]{3,2,1,0:T(8,128)(2,1)}, s32[1]{0:T(128)}, s32[2]{0:T(128)S(1)}) custom-call(s32[16]{0:T(128)S(1)} %copy-done.6, bf16[2,1744,128]{2,1,0:T(8,128)(2,1)S(1)} %get-tuple-element.57.sent_a, bf16[2,1744,128]{2,1,0:T(8,128)(2,1)S(1)} %get-tuple-element.58.sent_b, ...), custom_call_target="tpu_custom_call", output_to_operand_aliasing={{0}: (5, {})} | custom-call | tf_op jit(solution)/shard_map/place/pallas_call | solution.py:312
  (9 shorter events, 0.1 us)
Async XLA Ops:
  0.6 9.9 %copy-start.5 = (s32[16]{0:T(128)S(1)}, s32[16]{0:T(128)}, u32[]{:S(2)}) copy-start(s32[16]{0:T(128)} %len_in.3) | copy-start | bytes 196
  0.6 9.9 %copy-start.4 = (bf16[16,4,128]{2,1,0:T(4,128)(2,1)S(1)}, bf16[16,4,128]{2,1,0:T(4,128)(2,1)}, u32[]{:S(2)}) copy-start(bf16[16,4,128]{2,1,0:T(4,128)(2,1)} %nv_hbm.1) | copy-start | bytes 49156
  0.7 9.9 %copy-start.3 = (bf16[16,4,128]{2,1,0:T(4,128)(2,1)S(1)}, bf16[16,4,128]{2,1,0:T(4,128)(2,1)}, u32[]{:S(2)}) copy-start(bf16[16,4,128]{2,1,0:T(4,128)(2,1)} %nk_hbm.1) | copy-start | bytes 49156
  0.7 9.8 %copy-start.1 = (bf16[2048,128]{1,0:T(8,128)(2,1)S(1)}, bf16[2048,128]{1,0:T(8,128)(2,1)}, u32[]{:S(2)}) copy-start(bf16[2048,128]{1,0:T(8,128)(2,1)} %pv_ref.1) | copy-start | bytes 1572868
  0.7 9.8 %copy-start = (bf16[2048,128]{1,0:T(8,128)(2,1)S(1)}, bf16[2048,128]{1,0:T(8,128)(2,1)}, u32[]{:S(2)}) copy-start(bf16[2048,128]{1,0:T(8,128)(2,1)} %pk_ref.1) | copy-start | bytes 1572868
  0.7 9.8 %copy-start.2 = (bf16[16,4,1024]{2,1,0:T(4,128)(2,1)S(1)}, bf16[16,4,1024]{2,1,0:T(4,128)(2,1)}, u32[]{:S(2)}) copy-start(bf16[16,4,1024]{2,1,0:T(4,128)(2,1)} %q_ref.1) | copy-start | bytes 393220
  3.3 26.1 %collective-permute-start.6 = (bf16[2,1744,128]{2,1,0:T(8,128)(2,1)S(1)}, bf16[2,1744,128]{2,1,0:T(8,128)(2,1)S(1)}, u32[]{:S(2)}, u32[]{:S(2)}) collective-permute-start(bf16[2,1744,128]{2,1,0:T(8,128)(2,1)S(1)} %get-tuple-element.57.sent_a), channel_id=1, source_target_pairs={{0,8},{1,9},{2,10},{3,11},{4,12},{5,13},{6,14},{7,15},{8,0},{9,1},... | collective-permute-start | bytes 2678792 | tf_op jit(solution)/shard_map/ppermute | solution.py:599
  5.3 18.9 %copy-start.6 = (s32[16]{0:T(128)S(1)}, s32[16]{0:T(128)}, u32[]{:S(2)}) copy-start(s32[16]{0:T(128)} %anc_in.3) | copy-start | bytes 196
  5.3 24.7 %collective-permute-start.7 = (bf16[2,1744,128]{2,1,0:T(8,128)(2,1)S(1)}, bf16[2,1744,128]{2,1,0:T(8,128)(2,1)S(1)}, u32[]{:S(2)}, u32[]{:S(2)}) collective-permute-start(bf16[2,1744,128]{2,1,0:T(8,128)(2,1)S(1)} %get-tuple-element.58.sent_b), channel_id=1, source_target_pairs={{0,1},{1,0},{2,3},{3,2},{4,5},{5,4},{6,7},{7,6},{8,16},{9,17},{10,... | collective-permute-start | bytes 2678792 | tf_op jit(solution)/shard_map/ppermute | solution.py:599
  17.2 1.6 %collective-permute-start.2 = (bf16[4,64,512]{2,1,0:T(8,128)(2,1)S(1)}, bf16[4,64,512]{2,1,0:T(8,128)(2,1)S(1)}, u32[]{:S(2)}, u32[]{:S(2)}) collective-permute-start(bf16[4,64,512]{2,1,0:T(8,128)(2,1)S(1)} %get-tuple-element.52), channel_id=1, source_target_pairs={{0,1},{1,0},{2,3},{3,2},{4,5},{5,4},{6,7},{7,6},{8,9},{9,8},{10,11... | collective-permute-start | bytes 786440 | tf_op jit(solution)/shard_map/ppermute | solution.py:605
  18.9 7.5 %collective-permute-start.3 = (bf16[64,512]{1,0:T(8,128)(2,1)S(1)}, bf16[64,512]{1,0:T(8,128)(2,1)S(1)}, u32[]{:S(2)}, u32[]{:S(2)}) collective-permute-start(bf16[64,512]{1,0:T(8,128)(2,1)S(1)} %get-tuple-element.54), channel_id=1, source_target_pairs={{0,4},{1,5},{2,6},{3,7},{4,0},{5,1},{6,2},{7,3},{8,12},{9,13},{10,... | collective-permute-start | bytes 196616 | tf_op jit(solution)/shard_map/ppermute | solution.py:608
  22.2 4.3 %collective-permute-start.4 = (bf16[64,512]{1,0:T(8,128)(2,1)S(1)}, bf16[64,512]{1,0:T(8,128)(2,1)S(1)}, u32[]{:S(2)}, u32[]{:S(2)}) collective-permute-start(bf16[64,512]{1,0:T(8,128)(2,1)S(1)} %get-tuple-element.55), channel_id=1, source_target_pairs={{0,6},{1,7},{2,0},{3,1},{4,2},{5,3},{6,4},{7,5},{8,14},{9,15},{10,... | collective-permute-start | bytes 196616 | tf_op jit(solution)/shard_map/ppermute | solution.py:608
  23.2 5.5 %collective-permute-start.5 = (bf16[64,512]{1,0:T(8,128)(2,1)S(1)}, bf16[64,512]{1,0:T(8,128)(2,1)S(1)}, u32[]{:S(2)}, u32[]{:S(2)}) collective-permute-start(bf16[64,512]{1,0:T(8,128)(2,1)S(1)} %get-tuple-element.56), channel_id=1, source_target_pairs={{0,2},{1,3},{2,4},{3,5},{4,6},{5,7},{6,0},{7,1},{8,10},{9,11},{10,... | collective-permute-start | bytes 196616 | tf_op jit(solution)/shard_map/ppermute | solution.py:608

commit v4 on v3

--- a/solution.py
+++ b/solution.py
@@ -127,10 +127,16 @@
         copy.wait()
 
     def renew(target, place, p, count):
-        for kv, fresh_ref in ((0, nk), (1, nv)):
-            fresh = fresh_ref[p].astype(F32)
-            for tile in (jnp.maximum(count - 2, 0), count - 1):
+        def one(tile):
+            for kv, fresh_ref in ((0, nk), (1, nv)):
+                fresh = fresh_ref[p].astype(F32)
                 insert(target, (kv, tile_at(place + tile)), tile, lens[p], fresh, steps)
+
+        one(count - 1)
+
+        @pl.when(lens[p] < (count - 1) * TILE)
+        def _():
+            one(count - 2)
 
     for fits, copy, p, count, place, head in spots():
 
@@ -269,8 +275,8 @@
 
 
 def place_kernel(
-    steps, anc_in, sent_a, sent_b, head_a, head_b, held_ref, out_ref, any_ref, more_ref,
-    ancs, lens, places, header, own, header_sems, live_sems,
+    steps, anc_in, sent_a, sent_b, head_a, head_b, held_ref, out_ref, any_out,
+    any_ref, ancs, lens, places, header, own, header_sems, live_sems, any_sem,
 ):
     del held_ref
     rows, _, slots, _ = out_ref.shape
@@ -300,10 +306,12 @@
     each(lambda copy: copy.start())
     flag = rows // 2
     both = jnp.maximum(header[...].astype(F32), own[...].astype(F32))
-    for side in range(2):
-        more_ref[side] = jnp.max(both[side, flag : flag + 1]).astype(jnp.int32)
-    any_ref[0] = jnp.maximum(more_ref[0], more_ref[1])
+    both = jnp.maximum(both[0, flag : flag + 1], both[1, flag : flag + 1])
+    any_ref[0] = jnp.max(both).astype(jnp.int32)
+    tell = pltpu.make_async_copy(any_ref, any_out, any_sem.at[0])
+    tell.start()
     each(lambda copy: copy.wait())
+    tell.wait()
 
 
 def place(steps, ancestors, sent, heads, held):
@@ -314,11 +322,11 @@
         out_shape=(
             like(held),
             jax.ShapeDtypeStruct((1,), jnp.int32),
-            jax.ShapeDtypeStruct((2,), jnp.int32),
         ),
         in_specs=[ANY] * 5 + [HBM],
-        out_specs=(HBM, SMEM, SMEM),
+        out_specs=(HBM, HBM),
         scratch_shapes=[
+            pltpu.SMEM((1,), jnp.int32),
             pltpu.SMEM((rows,), jnp.int32),
             pltpu.SMEM((2, half), jnp.int32),
             pltpu.SMEM((2, half), jnp.int32),
@@ -326,6 +334,7 @@
             pltpu.VMEM((2, TILE, hd), BF16),
             pltpu.SemaphoreType.DMA((5,)),
             pltpu.SemaphoreType.DMA((rows,)),
+            pltpu.SemaphoreType.DMA((1,)),
         ],
         input_output_aliases={5: 0},
         compiler_params=params(1),
@@ -611,14 +620,18 @@
     mixed = chip_sum(mine, arrived, rows)
     held = keep(steps, lengths, ancestors, app)
 
-    held, some, more = place(steps, ancestors, packed[:2], heads, held)
+    held, some = place(steps, ancestors, packed[:2], heads, held)
 
     def exchange(held, *tails):
+        more = [
+            jnp.maximum(sent[0, rows // 2, 0], got[0, rows // 2, 0])
+            for sent, got in zip(packed[:2], heads)
+        ]
         got = [
             lax.cond(
                 flag > 0, lambda v, route=route: lax.ppermute(v, ("dom", "tp"), route), lambda v: v, tail
             )
-            for flag, tail, route in zip((more[0], more[1]), tails, routes)
+            for flag, tail, route in zip(more, tails, routes)
         ]
         return place_tails(steps, ancestors, heads, got, held)
 

time: 33.2 us -> 32.5 us (0.979)
  Pallas kernels: 14.5 us -> 13.9 us
    pallas_call x1, Pallas kernels: 2.37 us -> 1.83 us  [place(): pl.pallas_call(functools.partial(place_kernel, steps), out_shape=(like(he...]
  transfers between devices with their start and end apart: 6 -> 6, of which waited for: 4 -> 4; matrix products, arithmetic and copies ran while one was open for 0% -> 0% of each run, Pallas kernels for 29% -> 30%
where the time goes in v4:
time: 32.5 us; the launch traced here: 32.4 us
  Pallas kernels  13.9 us (43%)
  starting transfers between devices  12.6 us (39%)
  waiting for transfers between devices  4.47 us (14%)
  between operations  1.39 us (4%)
    ppermute x2, starting transfers between devices, body(): lax.ppermute(head, ('dom', 'tp'), route)  7.19 us
    pallas_call x1, Pallas kernels, attend(): pl.pallas_call(attend_kernel, out_shape=(jax.ShapeDtypeStruct((chips, tok...  6.7 us
    ppermute x3, starting transfers between devices, body(): lax.ppermute(send[k - 1], 'tp', [(i, (i + 2 * k) % tps) for i in range(tp...  5.31 us
    pallas_call x1, Pallas kernels, first(): pl.pallas_call(first_kernel, out_shape=(head, head, tail, tail), in_specs...  2.49 us
    ppermute x3, waiting for transfers between devices, body(): lax.ppermute(send[k - 1], 'tp', [(i, (i + 2 * k) % tps) for i in range(tp...  2.31 us
    pallas_call x1, Pallas kernels, keep(): pl.pallas_call(functools.partial(keep_kernel, steps), out_shape=like(app)...  2.18 us
    pallas_call x1, Pallas kernels, place(): pl.pallas_call(functools.partial(place_kernel, steps), out_shape=(like(he...  1.83 us
    ppermute x1, waiting for transfers between devices, body(): got = lax.ppermute(theirs, 'tp', [(i, i ^ 1) for i in range(tps)])  1.52 us
  transfers between devices with their start and end apart: 6, of which 4 were waited for; matrix products, arithmetic and copies ran while one was open for 0% of the time, Pallas kernels for 30%

profile of v4, /device:TPU:6, one launch (start us, length us, event | category | flops | bytes accessed | tf_op | source)
XLA Modules:
  0.0 32.4 jit_solution(16008978870460115864)
XLA Ops:
  0.6 0.0 copy-start.5
  0.6 0.0 copy-start.4
  0.7 0.0 copy-start.3
  0.7 0.0 copy-start.1
  0.7 2.5 %first.1 = (bf16[2,1744,128]{2,1,0:T(8,128)(2,1)S(1)}, bf16[2,1744,128]{2,1,0:T(8,128)(2,1)S(1)}, bf16[2,560,128]{2,1,0:T(8,128)(2,1)S(1)}, bf16[2,560,128]{2,1,0:T(8,128)(2,1)S(1)}) custom-call(s32[16]{0:T(128)} %len_in.3, bf16[16,2,256,128]{3,2,1,0:T(8,128)(2,1)} %cache_ref.3, bf16[16,4,128]{2,1,0:T(4,128)(2,1)} %nk_hbm.1, bf16[16,4,128]{2,1,0:T(4,128)(2,1)} %nv_hbm.1), custom_call_target="tpu_custom_call" | custom-call | tf_op jit(solution)/shard_map/first/pallas_call | solution.py:175
  3.2 2.0 %collective-permute-start.6 = (bf16[2,1744,128]{2,1,0:T(8,128)(2,1)S(1)}, bf16[2,1744,128]{2,1,0:T(8,128)(2,1)S(1)}, u32[]{:S(2)}, u32[]{:S(2)}) collective-permute-start(bf16[2,1744,128]{2,1,0:T(8,128)(2,1)S(1)} %get-tuple-element.59.sent_a), channel_id=1, source_target_pairs={{0,8},{1,9},{2,10},{3,11},{4,12},{5,13},{6,14},{7,15},{8,0},{9,1},... | collective-permute-start | bytes 2678792 | tf_op jit(solution)/shard_map/ppermute | solution.py:608
  5.2 5.2 %collective-permute-start.7 = (bf16[2,1744,128]{2,1,0:T(8,128)(2,1)S(1)}, bf16[2,1744,128]{2,1,0:T(8,128)(2,1)S(1)}, u32[]{:S(2)}, u32[]{:S(2)}) collective-permute-start(bf16[2,1744,128]{2,1,0:T(8,128)(2,1)S(1)} %get-tuple-element.60.sent_b), channel_id=1, source_target_pairs={{0,1},{1,0},{2,3},{3,2},{4,5},{5,4},{6,7},{7,6},{8,16},{9,17},{10,... | collective-permute-start | bytes 2678792 | tf_op jit(solution)/shard_map/ppermute | solution.py:608
  10.4 0.0 copy-done.5
  10.4 0.0 copy-done
  10.4 0.0 copy-done.2
  10.4 6.7 %attend.1 = (bf16[4,64,512]{2,1,0:T(8,128)(2,1)S(1)}, f32[4,64,512]{2,1,0:T(8,128)S(1)}, bf16[16,2,256,128]{3,2,1,0:T(8,128)(2,1)S(1)}) custom-call(s32[16]{0:T(128)S(1)} %copy-done.5, bf16[16,2,256,128]{3,2,1,0:T(8,128)(2,1)} %cache_ref.3, bf16[16,4,128]{2,1,0:T(4,128)(2,1)S(1)} %copy-done.3, bf16[16,4,128]{2,1,0:T(4,128)(2,1)S(1)} %copy-done.4, ...), custom_call_target="tpu_custom_call" | custom-call | flops 1073741824 | bytes 8388608 | tf_op jit(solution)/shard_map/attend/pallas_call | solution.py:505
  17.1 0.1 collective-permute-start.2
  17.2 1.5 %collective-permute-done.2.got_ref = bf16[4,64,512]{2,1,0:T(8,128)(2,1)S(1)} collective-permute-done((bf16[4,64,512]{2,1,0:T(8,128)(2,1)S(1)}, bf16[4,64,512]{2,1,0:T(8,128)(2,1)S(1)}, u32[]{:S(2)}, u32[]{:S(2)}) %collective-permute-start.2) | collective-permute-done | bytes 262176 | tf_op jit(solution)/shard_map/ppermute | solution.py:614
  18.8 3.3 %collective-permute-start.3 = (bf16[64,512]{1,0:T(8,128)(2,1)S(1)}, bf16[64,512]{1,0:T(8,128)(2,1)S(1)}, u32[]{:S(2)}, u32[]{:S(2)}) collective-permute-start(bf16[64,512]{1,0:T(8,128)(2,1)S(1)} %get-tuple-element.56), channel_id=1, source_target_pairs={{0,4},{1,5},{2,6},{3,7},{4,0},{5,1},{6,2},{7,3},{8,12},{9,13},{10,... | collective-permute-start | bytes 196616 | tf_op jit(solution)/shard_map/ppermute | solution.py:617
  22.1 1.1 %collective-permute-start.4 = (bf16[64,512]{1,0:T(8,128)(2,1)S(1)}, bf16[64,512]{1,0:T(8,128)(2,1)S(1)}, u32[]{:S(2)}, u32[]{:S(2)}) collective-permute-start(bf16[64,512]{1,0:T(8,128)(2,1)S(1)} %get-tuple-element.57), channel_id=1, source_target_pairs={{0,6},{1,7},{2,0},{3,1},{4,2},{5,3},{6,4},{7,5},{8,14},{9,15},{10,... | collective-permute-start | bytes 196616 | tf_op jit(solution)/shard_map/ppermute | solution.py:617
  23.1 1.0 %collective-permute-start.5 = (bf16[64,512]{1,0:T(8,128)(2,1)S(1)}, bf16[64,512]{1,0:T(8,128)(2,1)S(1)}, u32[]{:S(2)}, u32[]{:S(2)}) collective-permute-start(bf16[64,512]{1,0:T(8,128)(2,1)S(1)} %get-tuple-element.58), channel_id=1, source_target_pairs={{0,2},{1,3},{2,4},{3,5},{4,6},{5,7},{6,0},{7,1},{8,10},{9,11},{10,... | collective-permute-start | bytes 196616 | tf_op jit(solution)/shard_map/ppermute | solution.py:617
  24.1 2.2 %keep.1.held_ref = bf16[16,2,256,128]{3,2,1,0:T(8,128)(2,1)} custom-call(s32[16]{0:T(128)S(1)} %copy-done.5, s32[16]{0:T(128)S(1)} %copy-done.6, bf16[16,2,256,128]{3,2,1,0:T(8,128)(2,1)S(1)} %get-tuple-element.61.app_ref), custom_call_target="tpu_custom_call" | custom-call | tf_op jit(solution)/shard_map/keep/pallas_call | solution.py:231
  26.3 0.0 collective-permute-done.3.refs_0_
  26.3 0.1 collective-permute-done.4.refs_1_
  26.4 2.2 %collective-permute-done.5.refs_2_ = bf16[64,512]{1,0:T(8,128)(2,1)S(1)} collective-permute-done((bf16[64,512]{1,0:T(8,128)(2,1)S(1)}, bf16[64,512]{1,0:T(8,128)(2,1)S(1)}, u32[]{:S(2)}, u32[]{:S(2)}) %collective-permute-start.5) | collective-permute-done | bytes 65568 | tf_op jit(solution)/shard_map/ppermute | solution.py:617
  28.6 0.7 %chip_sum.1 = bf16[16,4,512]{2,1,0:T(4,128)(2,1)} custom-call(f32[64,512]{1,0:T(8,128)S(1)} %get-tuple-element.55.keep_ref, bf16[64,512]{1,0:T(8,128)(2,1)S(1)} %collective-permute-done.3.refs_0_, bf16[64,512]{1,0:T(8,128)(2,1)S(1)} %collective-permute-done.4.refs_1_, bf16[64,512]{1,0:T(8,128)(2,1)S(1)} %collective-permute-done.5.refs_2_), custom_call_target="tpu_custom_call" | custom-call | tf_op jit(solution)/shard_map/chip_sum/pallas_call | solution.py:574
  29.3 0.0 collective-permute-done.6.head_a
  29.3 0.6 %collective-permute-done.7.head_b = bf16[2,1744,128]{2,1,0:T(8,128)(2,1)S(1)} collective-permute-done((bf16[2,1744,128]{2,1,0:T(8,128)(2,1)S(1)}, bf16[2,1744,128]{2,1,0:T(8,128)(2,1)S(1)}, u32[]{:S(2)}, u32[]{:S(2)}) %collective-permute-start.7) | collective-permute-done | bytes 892960 | tf_op jit(solution)/shard_map/ppermute | solution.py:608
  29.9 1.8 %place.1 = (bf16[16,2,256,128]{3,2,1,0:T(8,128)(2,1)}, s32[1]{0:T(128)}) custom-call(s32[16]{0:T(128)S(1)} %copy-done.6, bf16[2,1744,128]{2,1,0:T(8,128)(2,1)S(1)} %get-tuple-element.59.sent_a, bf16[2,1744,128]{2,1,0:T(8,128)(2,1)S(1)} %get-tuple-element.60.sent_b, ...), custom_call_target="tpu_custom_call", output_to_operand_aliasing={{0}: (5, {})} | custom-call | tf_op jit(solution)/shard_map/place/pallas_call | solution.py:320
  (9 shorter events, 0.1 us)
Async XLA Ops:
  0.6 9.8 %copy-start.5 = (s32[16]{0:T(128)S(1)}, s32[16]{0:T(128)}, u32[]{:S(2)}) copy-start(s32[16]{0:T(128)} %len_in.3) | copy-start | bytes 196
  0.6 9.7 %copy-start.4 = (bf16[16,4,128]{2,1,0:T(4,128)(2,1)S(1)}, bf16[16,4,128]{2,1,0:T(4,128)(2,1)}, u32[]{:S(2)}) copy-start(bf16[16,4,128]{2,1,0:T(4,128)(2,1)} %nv_hbm.1) | copy-start | bytes 49156
  0.7 9.7 %copy-start.3 = (bf16[16,4,128]{2,1,0:T(4,128)(2,1)S(1)}, bf16[16,4,128]{2,1,0:T(4,128)(2,1)}, u32[]{:S(2)}) copy-start(bf16[16,4,128]{2,1,0:T(4,128)(2,1)} %nk_hbm.1) | copy-start | bytes 49156
  0.7 9.7 %copy-start.1 = (bf16[2048,128]{1,0:T(8,128)(2,1)S(1)}, bf16[2048,128]{1,0:T(8,128)(2,1)}, u32[]{:S(2)}) copy-start(bf16[2048,128]{1,0:T(8,128)(2,1)} %pv_ref.1) | copy-start | bytes 1572868
  0.7 9.7 %copy-start = (bf16[2048,128]{1,0:T(8,128)(2,1)S(1)}, bf16[2048,128]{1,0:T(8,128)(2,1)}, u32[]{:S(2)}) copy-start(bf16[2048,128]{1,0:T(8,128)(2,1)} %pk_ref.1) | copy-start | bytes 1572868
  0.7 9.7 %copy-start.2 = (bf16[16,4,1024]{2,1,0:T(4,128)(2,1)S(1)}, bf16[16,4,1024]{2,1,0:T(4,128)(2,1)}, u32[]{:S(2)}) copy-start(bf16[16,4,1024]{2,1,0:T(4,128)(2,1)} %q_ref.1) | copy-start | bytes 393220
  3.2 26.1 %collective-permute-start.6 = (bf16[2,1744,128]{2,1,0:T(8,128)(2,1)S(1)}, bf16[2,1744,128]{2,1,0:T(8,128)(2,1)S(1)}, u32[]{:S(2)}, u32[]{:S(2)}) collective-permute-start(bf16[2,1744,128]{2,1,0:T(8,128)(2,1)S(1)} %get-tuple-element.59.sent_a), channel_id=1, source_target_pairs={{0,8},{1,9},{2,10},{3,11},{4,12},{5,13},{6,14},{7,15},{8,0},{9,1},... | collective-permute-start | bytes 2678792 | tf_op jit(solution)/shard_map/ppermute | solution.py:608
  5.2 18.9 %copy-start.6 = (s32[16]{0:T(128)S(1)}, s32[16]{0:T(128)}, u32[]{:S(2)}) copy-start(s32[16]{0:T(128)} %anc_in.3) | copy-start | bytes 196
  5.2 24.7 %collective-permute-start.7 = (bf16[2,1744,128]{2,1,0:T(8,128)(2,1)S(1)}, bf16[2,1744,128]{2,1,0:T(8,128)(2,1)S(1)}, u32[]{:S(2)}, u32[]{:S(2)}) collective-permute-start(bf16[2,1744,128]{2,1,0:T(8,128)(2,1)S(1)} %get-tuple-element.60.sent_b), channel_id=1, source_target_pairs={{0,1},{1,0},{2,3},{3,2},{4,5},{5,4},{6,7},{7,6},{8,16},{9,17},{10,... | collective-permute-start | bytes 2678792 | tf_op jit(solution)/shard_map/ppermute | solution.py:608
  17.1 1.6 %collective-permute-start.2 = (bf16[4,64,512]{2,1,0:T(8,128)(2,1)S(1)}, bf16[4,64,512]{2,1,0:T(8,128)(2,1)S(1)}, u32[]{:S(2)}, u32[]{:S(2)}) collective-permute-start(bf16[4,64,512]{2,1,0:T(8,128)(2,1)S(1)} %get-tuple-element.54), channel_id=1, source_target_pairs={{0,1},{1,0},{2,3},{3,2},{4,5},{5,4},{6,7},{7,6},{8,9},{9,8},{10,11... | collective-permute-start | bytes 786440 | tf_op jit(solution)/shard_map/ppermute | solution.py:614
  18.8 7.5 %collective-permute-start.3 = (bf16[64,512]{1,0:T(8,128)(2,1)S(1)}, bf16[64,512]{1,0:T(8,128)(2,1)S(1)}, u32[]{:S(2)}, u32[]{:S(2)}) collective-permute-start(bf16[64,512]{1,0:T(8,128)(2,1)S(1)} %get-tuple-element.56), channel_id=1, source_target_pairs={{0,4},{1,5},{2,6},{3,7},{4,0},{5,1},{6,2},{7,3},{8,12},{9,13},{10,... | collective-permute-start | bytes 196616 | tf_op jit(solution)/shard_map/ppermute | solution.py:617
  22.1 4.3 %collective-permute-start.4 = (bf16[64,512]{1,0:T(8,128)(2,1)S(1)}, bf16[64,512]{1,0:T(8,128)(2,1)S(1)}, u32[]{:S(2)}, u32[]{:S(2)}) collective-permute-start(bf16[64,512]{1,0:T(8,128)(2,1)S(1)} %get-tuple-element.57), channel_id=1, source_target_pairs={{0,6},{1,7},{2,0},{3,1},{4,2},{5,3},{6,4},{7,5},{8,14},{9,15},{10,... | collective-permute-start | bytes 196616 | tf_op jit(solution)/shard_map/ppermute | solution.py:617
  23.1 5.5 %collective-permute-start.5 = (bf16[64,512]{1,0:T(8,128)(2,1)S(1)}, bf16[64,512]{1,0:T(8,128)(2,1)S(1)}, u32[]{:S(2)}, u32[]{:S(2)}) collective-permute-start(bf16[64,512]{1,0:T(8,128)(2,1)S(1)} %get-tuple-element.58), channel_id=1, source_target_pairs={{0,2},{1,3},{2,4},{3,5},{4,6},{5,7},{6,0},{7,1},{8,10},{9,11},{10,... | collective-permute-start | bytes 196616 | tf_op jit(solution)/shard_map/ppermute | solution.py:617

commit v5 on v4

--- a/solution.py
+++ b/solution.py
@@ -396,8 +396,8 @@
 
 
 def attend_kernel(
-    len_in, cache_ref, nk_in, nv_in, q_ref, pk_ref, pv_ref, w_ref, theirs_ref, ours_ref, app_ref,
-    len_ref, nk, nv, small_sems, in_sems, qs, att, wbuf, sems,
+    len_in, cache_ref, nk_in, nv_in, q_in, pk_in, pv_in, w_ref, theirs_ref, ours_ref, app_ref,
+    len_ref, nk, nv, q_ref, pk_ref, pv_ref, small_sems, in_sems, qs, att, wbuf, sems,
 ):
     rows, steps, _ = q_ref.shape
     heads = q_ref.shape[2] // HD
@@ -410,6 +410,14 @@
         cols = pl.ds(pl.multiple_of((2 * lax.rem(k, chips) + who) * width, width), width)
         return pltpu.make_async_copy(w_ref.at[:, cols], wbuf.at[k], sems.at[k])
 
+    sources = (len_in, nk_in, nv_in, q_in, pk_in, pv_in)
+    targets = (len_ref, nk, nv, q_ref, pk_ref, pv_ref)
+    copies = [
+        pltpu.make_async_copy(a, b, small_sems.at[i]) for i, (a, b) in enumerate(zip(sources, targets))
+    ]
+    for copy in copies:
+        copy.start()
+
     @pl.loop(0, rows)
     def _(p):
         pltpu.make_async_copy(cache_ref.at[p], app_ref.at[p], in_sems.at[p]).start()
@@ -418,7 +426,8 @@
     def _(k):
         w_copy(k).start()
 
-    load_all((len_in, nk_in, nv_in), (len_ref, nk, nv), small_sems)
+    for copy in copies:
+        copy.wait()
 
     pair = 2 * steps
     groups = rows // 2
@@ -509,13 +518,16 @@
             jax.ShapeDtypeStruct((chips, tokens, width), F32),
             like(cache),
         ),
-        in_specs=[ANY, HBM, ANY, ANY, VMEM, VMEM, VMEM, HBM],
+        in_specs=[HBM] * 8,
         out_specs=(VMEM, VMEM, VMEM),
         scratch_shapes=[
             pltpu.SMEM((rows,), jnp.int32),
             pltpu.VMEM(new_keys.shape, BF16),
             pltpu.VMEM(new_values.shape, BF16),
-            pltpu.SemaphoreType.DMA((3,)),
+            pltpu.VMEM(queries.shape, BF16),
+            pltpu.VMEM(prompt_keys.shape, BF16),
+            pltpu.VMEM(prompt_values.shape, BF16),
+            pltpu.SemaphoreType.DMA((6,)),
             pltpu.SemaphoreType.DMA((rows,)),
             pltpu.VMEM((tokens * q_cols // HD, HD), F32),
             pltpu.VMEM((tokens, q_cols), F32),
@@ -528,8 +540,12 @@
         ),
         name="attend",
     )(
-        lengths, in_hbm(cache), new_keys, new_values, queries, prompt_keys, prompt_values,
-        in_hbm(out_weight),
+        *map(
+            in_hbm,
+            (
+                lengths, cache, new_keys, new_values, queries, prompt_keys, prompt_values, out_weight,
+            ),
+        )
     )
 
 

time: 32.5 us -> 32.3 us (level)
  transfers between devices with their start and end apart: 6 -> 6, of which waited for: 4 -> 4; matrix products, arithmetic and copies ran while one was open for 0% -> 0% of each run, Pallas kernels for 30% -> 31%
where the time goes in v5:
time: 32.3 us; the launch traced here: 32.1 us
  Pallas kernels  14.1 us (44%)
  starting transfers between devices  12.6 us (39%)
  waiting for transfers between devices  4.23 us (13%)
  between operations  1.23 us (4%)
    ppermute x2, starting transfers between devices, body(): lax.ppermute(head, ('dom', 'tp'), route)  7.15 us
    pallas_call x1, Pallas kernels, attend(): pl.pallas_call(attend_kernel, out_shape=(jax.ShapeDtypeStruct((chips, tok...  6.97 us
    ppermute x3, starting transfers between devices, body(): lax.ppermute(send[k - 1], 'tp', [(i, (i + 2 * k) % tps) for i in range(tp...  5.31 us
    pallas_call x1, Pallas kernels, first(): pl.pallas_call(first_kernel, out_shape=(head, head, tail, tail), in_specs...  2.37 us
    ppermute x3, waiting for transfers between devices, body(): lax.ppermute(send[k - 1], 'tp', [(i, (i + 2 * k) % tps) for i in range(tp...  2.31 us
    pallas_call x1, Pallas kernels, keep(): pl.pallas_call(functools.partial(keep_kernel, steps), out_shape=like(app)...  2.17 us
    pallas_call x1, Pallas kernels, place(): pl.pallas_call(functools.partial(place_kernel, steps), out_shape=(like(he...  1.87 us
    ppermute x1, waiting for transfers between devices, body(): got = lax.ppermute(theirs, 'tp', [(i, i ^ 1) for i in range(tps)])  1.52 us
  transfers between devices with their start and end apart: 6, of which 4 were waited for; matrix products, arithmetic and copies ran while one was open for 0% of the time, Pallas kernels for 31%

profile of v5, /device:TPU:6, one launch (start us, length us, event | category | flops | bytes accessed | tf_op | source)
XLA Modules:
  0.0 32.1 jit_solution(16457544787937825431)
XLA Ops:
  0.6 2.4 %first.1 = (bf16[2,1744,128]{2,1,0:T(8,128)(2,1)S(1)}, bf16[2,1744,128]{2,1,0:T(8,128)(2,1)S(1)}, bf16[2,560,128]{2,1,0:T(8,128)(2,1)S(1)}, bf16[2,560,128]{2,1,0:T(8,128)(2,1)S(1)}) custom-call(s32[16]{0:T(128)} %len_in.3, bf16[16,2,256,128]{3,2,1,0:T(8,128)(2,1)} %cache_ref.3, bf16[16,4,128]{2,1,0:T(4,128)(2,1)} %nk_hbm.1, bf16[16,4,128]{2,1,0:T(4,128)(2,1)} %nv_hbm.1), custom_call_target="tpu_custom_call" | custom-call | tf_op jit(solution)/shard_map/first/pallas_call | solution.py:175
  3.0 2.0 %collective-permute-start.6 = (bf16[2,1744,128]{2,1,0:T(8,128)(2,1)S(1)}, bf16[2,1744,128]{2,1,0:T(8,128)(2,1)S(1)}, u32[]{:S(2)}, u32[]{:S(2)}) collective-permute-start(bf16[2,1744,128]{2,1,0:T(8,128)(2,1)S(1)} %get-tuple-element.59.sent_a), channel_id=1, source_target_pairs={{0,8},{1,9},{2,10},{3,11},{4,12},{5,13},{6,14},{7,15},{8,0},{9,1},... | collective-permute-start | bytes 2678792 | tf_op jit(solution)/shard_map/ppermute | solution.py:624
  5.0 0.0 copy-start
  5.0 0.0 copy-start.1
  5.0 5.2 %collective-permute-start.7 = (bf16[2,1744,128]{2,1,0:T(8,128)(2,1)S(1)}, bf16[2,1744,128]{2,1,0:T(8,128)(2,1)S(1)}, u32[]{:S(2)}, u32[]{:S(2)}) collective-permute-start(bf16[2,1744,128]{2,1,0:T(8,128)(2,1)S(1)} %get-tuple-element.60.sent_b), channel_id=1, source_target_pairs={{0,1},{1,0},{2,3},{3,2},{4,5},{5,4},{6,7},{7,6},{8,16},{9,17},{10,... | collective-permute-start | bytes 2678792 | tf_op jit(solution)/shard_map/ppermute | solution.py:624
  10.2 7.0 %attend.1 = (bf16[4,64,512]{2,1,0:T(8,128)(2,1)S(1)}, f32[4,64,512]{2,1,0:T(8,128)S(1)}, bf16[16,2,256,128]{3,2,1,0:T(8,128)(2,1)S(1)}) custom-call(s32[16]{0:T(128)} %len_in.3, bf16[16,2,256,128]{3,2,1,0:T(8,128)(2,1)} %cache_ref.3, bf16[16,4,128]{2,1,0:T(4,128)(2,1)} %nk_hbm.1, bf16[16,4,128]{2,1,0:T(4,128)(2,1)} %nv_hbm.1, bf16[16,4,1024]{2,1,0:T(4,128)(2,1)} %q_in.1, ...), custom_call_target="tpu_custom_call" | custom-call | flops 1073741824 | bytes 8388608 | tf_op jit(solution)/shard_map/attend/pallas_call | solution.py:514
  17.1 0.1 collective-permute-start.2
  17.2 1.5 %collective-permute-done.2.got_ref = bf16[4,64,512]{2,1,0:T(8,128)(2,1)S(1)} collective-permute-done((bf16[4,64,512]{2,1,0:T(8,128)(2,1)S(1)}, bf16[4,64,512]{2,1,0:T(8,128)(2,1)S(1)}, u32[]{:S(2)}, u32[]{:S(2)}) %collective-permute-start.2) | collective-permute-done | bytes 262176 | tf_op jit(solution)/shard_map/ppermute | solution.py:630
  18.8 0.1 pair_sum.1
  18.8 3.3 %collective-permute-start.3 = (bf16[64,512]{1,0:T(8,128)(2,1)S(1)}, bf16[64,512]{1,0:T(8,128)(2,1)S(1)}, u32[]{:S(2)}, u32[]{:S(2)}) collective-permute-start(bf16[64,512]{1,0:T(8,128)(2,1)S(1)} %get-tuple-element.56), channel_id=1, source_target_pairs={{0,4},{1,5},{2,6},{3,7},{4,0},{5,1},{6,2},{7,3},{8,12},{9,13},{10,... | collective-permute-start | bytes 196616 | tf_op jit(solution)/shard_map/ppermute | solution.py:633
  22.1 1.1 %collective-permute-start.4 = (bf16[64,512]{1,0:T(8,128)(2,1)S(1)}, bf16[64,512]{1,0:T(8,128)(2,1)S(1)}, u32[]{:S(2)}, u32[]{:S(2)}) collective-permute-start(bf16[64,512]{1,0:T(8,128)(2,1)S(1)} %get-tuple-element.57), channel_id=1, source_target_pairs={{0,6},{1,7},{2,0},{3,1},{4,2},{5,3},{6,4},{7,5},{8,14},{9,15},{10,... | collective-permute-start | bytes 196616 | tf_op jit(solution)/shard_map/ppermute | solution.py:633
  23.2 1.0 %collective-permute-start.5 = (bf16[64,512]{1,0:T(8,128)(2,1)S(1)}, bf16[64,512]{1,0:T(8,128)(2,1)S(1)}, u32[]{:S(2)}, u32[]{:S(2)}) collective-permute-start(bf16[64,512]{1,0:T(8,128)(2,1)S(1)} %get-tuple-element.58), channel_id=1, source_target_pairs={{0,2},{1,3},{2,4},{3,5},{4,6},{5,7},{6,0},{7,1},{8,10},{9,11},{10,... | collective-permute-start | bytes 196616 | tf_op jit(solution)/shard_map/ppermute | solution.py:633
  24.1 0.0 copy-done
  24.1 0.0 copy-done.1
  24.1 2.2 %keep.1.held_ref = bf16[16,2,256,128]{3,2,1,0:T(8,128)(2,1)} custom-call(s32[16]{0:T(128)S(1)} %copy-done, s32[16]{0:T(128)S(1)} %copy-done.1, bf16[16,2,256,128]{3,2,1,0:T(8,128)(2,1)S(1)} %get-tuple-element.61.app_ref), custom_call_target="tpu_custom_call" | custom-call | tf_op jit(solution)/shard_map/keep/pallas_call | solution.py:231
  26.3 0.0 collective-permute-done.3.refs_0_
  26.3 0.1 collective-permute-done.4.refs_1_
  26.4 2.2 %collective-permute-done.5.refs_2_ = bf16[64,512]{1,0:T(8,128)(2,1)S(1)} collective-permute-done((bf16[64,512]{1,0:T(8,128)(2,1)S(1)}, bf16[64,512]{1,0:T(8,128)(2,1)S(1)}, u32[]{:S(2)}, u32[]{:S(2)}) %collective-permute-start.5) | collective-permute-done | bytes 65568 | tf_op jit(solution)/shard_map/ppermute | solution.py:633
  28.6 0.7 %chip_sum.1 = bf16[16,4,512]{2,1,0:T(4,128)(2,1)} custom-call(f32[64,512]{1,0:T(8,128)S(1)} %get-tuple-element.55.keep_ref, bf16[64,512]{1,0:T(8,128)(2,1)S(1)} %collective-permute-done.3.refs_0_, bf16[64,512]{1,0:T(8,128)(2,1)S(1)} %collective-permute-done.4.refs_1_, bf16[64,512]{1,0:T(8,128)(2,1)S(1)} %collective-permute-done.5.refs_2_), custom_call_target="tpu_custom_call" | custom-call | tf_op jit(solution)/shard_map/chip_sum/pallas_call | solution.py:590
  29.3 0.0 collective-permute-done.6.head_a
  29.3 0.4 %collective-permute-done.7.head_b = bf16[2,1744,128]{2,1,0:T(8,128)(2,1)S(1)} collective-permute-done((bf16[2,1744,128]{2,1,0:T(8,128)(2,1)S(1)}, bf16[2,1744,128]{2,1,0:T(8,128)(2,1)S(1)}, u32[]{:S(2)}, u32[]{:S(2)}) %collective-permute-start.7) | collective-permute-done | bytes 892960 | tf_op jit(solution)/shard_map/ppermute | solution.py:624
  29.7 1.9 %place.1 = (bf16[16,2,256,128]{3,2,1,0:T(8,128)(2,1)}, s32[1]{0:T(128)}) custom-call(s32[16]{0:T(128)S(1)} %copy-done.1, bf16[2,1744,128]{2,1,0:T(8,128)(2,1)S(1)} %get-tuple-element.59.sent_a, bf16[2,1744,128]{2,1,0:T(8,128)(2,1)S(1)} %get-tuple-element.60.sent_b, ...), custom_call_target="tpu_custom_call", output_to_operand_aliasing={{0}: (5, {})} | custom-call | tf_op jit(solution)/shard_map/place/pallas_call | solution.py:320
  (1 shorter events, 0.0 us)
Async XLA Ops:
  3.0 26.3 %collective-permute-start.6 = (bf16[2,1744,128]{2,1,0:T(8,128)(2,1)S(1)}, bf16[2,1744,128]{2,1,0:T(8,128)(2,1)S(1)}, u32[]{:S(2)}, u32[]{:S(2)}) collective-permute-start(bf16[2,1744,128]{2,1,0:T(8,128)(2,1)S(1)} %get-tuple-element.59.sent_a), channel_id=1, source_target_pairs={{0,8},{1,9},{2,10},{3,11},{4,12},{5,13},{6,14},{7,15},{8,0},{9,1},... | collective-permute-start | bytes 2678792 | tf_op jit(solution)/shard_map/ppermute | solution.py:624
  5.0 19.2 %copy-start = (s32[16]{0:T(128)S(1)}, s32[16]{0:T(128)}, u32[]{:S(2)}) copy-start(s32[16]{0:T(128)} %len_in.3) | copy-start | bytes 196
  5.0 19.2 %copy-start.1 = (s32[16]{0:T(128)S(1)}, s32[16]{0:T(128)}, u32[]{:S(2)}) copy-start(s32[16]{0:T(128)} %anc_in.3) | copy-start | bytes 196
  5.0 24.7 %collective-permute-start.7 = (bf16[2,1744,128]{2,1,0:T(8,128)(2,1)S(1)}, bf16[2,1744,128]{2,1,0:T(8,128)(2,1)S(1)}, u32[]{:S(2)}, u32[]{:S(2)}) collective-permute-start(bf16[2,1744,128]{2,1,0:T(8,128)(2,1)S(1)} %get-tuple-element.60.sent_b), channel_id=1, source_target_pairs={{0,1},{1,0},{2,3},{3,2},{4,5},{5,4},{6,7},{7,6},{8,16},{9,17},{10,... | collective-permute-start | bytes 2678792 | tf_op jit(solution)/shard_map/ppermute | solution.py:624
  17.1 1.6 %collective-permute-start.2 = (bf16[4,64,512]{2,1,0:T(8,128)(2,1)S(1)}, bf16[4,64,512]{2,1,0:T(8,128)(2,1)S(1)}, u32[]{:S(2)}, u32[]{:S(2)}) collective-permute-start(bf16[4,64,512]{2,1,0:T(8,128)(2,1)S(1)} %get-tuple-element.54), channel_id=1, source_target_pairs={{0,1},{1,0},{2,3},{3,2},{4,5},{5,4},{6,7},{7,6},{8,9},{9,8},{10,11... | collective-permute-start | bytes 786440 | tf_op jit(solution)/shard_map/ppermute | solution.py:630
  18.8 7.5 %collective-permute-start.3 = (bf16[64,512]{1,0:T(8,128)(2,1)S(1)}, bf16[64,512]{1,0:T(8,128)(2,1)S(1)}, u32[]{:S(2)}, u32[]{:S(2)}) collective-permute-start(bf16[64,512]{1,0:T(8,128)(2,1)S(1)} %get-tuple-element.56), channel_id=1, source_target_pairs={{0,4},{1,5},{2,6},{3,7},{4,0},{5,1},{6,2},{7,3},{8,12},{9,13},{10,... | collective-permute-start | bytes 196616 | tf_op jit(solution)/shard_map/ppermute | solution.py:633
  22.1 4.3 %collective-permute-start.4 = (bf16[64,512]{1,0:T(8,128)(2,1)S(1)}, bf16[64,512]{1,0:T(8,128)(2,1)S(1)}, u32[]{:S(2)}, u32[]{:S(2)}) collective-permute-start(bf16[64,512]{1,0:T(8,128)(2,1)S(1)} %get-tuple-element.57), channel_id=1, source_target_pairs={{0,6},{1,7},{2,0},{3,1},{4,2},{5,3},{6,4},{7,5},{8,14},{9,15},{10,... | collective-permute-start | bytes 196616 | tf_op jit(solution)/shard_map/ppermute | solution.py:633
  23.2 5.5 %collective-permute-start.5 = (bf16[64,512]{1,0:T(8,128)(2,1)S(1)}, bf16[64,512]{1,0:T(8,128)(2,1)S(1)}, u32[]{:S(2)}, u32[]{:S(2)}) collective-permute-start(bf16[64,512]{1,0:T(8,128)(2,1)S(1)} %get-tuple-element.58), channel_id=1, source_target_pairs={{0,2},{1,3},{2,4},{3,5},{4,6},{5,7},{6,0},{7,1},{8,10},{9,11},{10,... | collective-permute-start | bytes 196616 | tf_op jit(solution)/shard_map/ppermute | solution.py:633
